TPU v7x, 32 devices: a whole 2x2x4 slice. The times are simulated.
32 devices in a mesh: groups: 2 (over x), seq: 16 (over z, y, core).
Axes of the slice: x: 2, y: 2, z: 4, core: 2. Of those that a mesh axis runs over, the one named last changes fastest.
Arguments:
- inputs: bfloat16 [4, 8192, 768], P('groups', 'seq'), parts along dimension 0, may hold values from -6 to 6
- layer_norm_gain: float32 [768], replicated, may hold values from 0.1 to 1.9
- w_dilated: bfloat16 [3, 768, 384], replicated, may hold values from -0.125 to 0.125
- w_point: bfloat16 [384, 768], replicated, may hold values from -0.3125 to 0.3125
- cotangent: bfloat16 [4, 8192, 768], P('groups', 'seq'), parts along dimension 0, may hold values from -6 to 6
Outputs:
- outputs: bfloat16 [4, 8192, 768], P('groups', 'seq'), parts along dimension 0
- grad_inputs: bfloat16 [4, 8192, 768], P('groups', 'seq'), parts along dimension 0
- grad_dilated: float32 [6, 768, 384], P('groups', 'seq'), parts along dimension 0
- grad_point: float32 [768, 768], P('groups', 'seq'), parts along dimension 0
- grad_gain: float32 [1536], P(('groups', 'seq')), parts along dimension 0
There are 2 independent parts, one for each index of `groups`. A program takes and returns all parts, laid end to end along the dimension named above; an argument that names none is the same for every part. Nothing has to cross between parts.
All inputs are finite; a program needn't handle non-finite values.
Results may differ from a plain program's by a relative error of at most 0.0053.
Values may be sent and summed in bfloat16 or wider, within the bound.
A program may use at most 128 MiB of HBM per device.

v0:
```python
import jax
import jax.numpy as jnp
from jax import lax
from jax.sharding import PartitionSpec as P

HOPS = 8


def passed_along(value, axis, steps):
    count = lax.axis_size(axis)
    leading, last = (max(0, -steps), min(count, count - steps))
    return lax.ppermute(value, axis, [(source, source + steps) for source in range(leading, last)])


def gelu_fn(value):
    return jax.nn.gelu(value, approximate=True)


def gelu_back(value, upstream):
    return jax.vjp(gelu_fn, value)[1](upstream)[0]


def per_device(inputs, layer_norm_gain, w_dilated, w_point, cotangent):
    num_seqs, local_bins, channel_count = inputs.shape
    local_rows = num_seqs * local_bins
    row_total_count = local_rows * lax.axis_size("seq")
    x_float = inputs.astype(jnp.float32).reshape(local_rows, channel_count)
    middle_offset = x_float - jnp.mean(x_float, axis=-1, keepdims=True)
    inverse_deviation = lax.rsqrt(
        jnp.mean(middle_offset * middle_offset, axis=-1, keepdims=True) + 1e-05
    )
    standardized_input = middle_offset * inverse_deviation
    normalized_input = standardized_input * layer_norm_gain
    activated = gelu_fn(normalized_input).astype(jnp.bfloat16)
    earlier = passed_along(activated, "seq", HOPS)
    later = passed_along(activated, "seq", -HOPS)
    kernel_taps = (earlier, activated, later)
    pre = jnp.dot(activated, w_dilated[1], preferred_element_type=jnp.float32)
    pre = pre + jnp.dot(earlier, w_dilated[0], preferred_element_type=jnp.float32)
    pre = pre + jnp.dot(later, w_dilated[2], preferred_element_type=jnp.float32)
    hid = gelu_fn(pre).astype(jnp.bfloat16)
    outputs = (x_float + jnp.dot(hid, w_point, preferred_element_type=jnp.float32)).astype(
        jnp.bfloat16
    )
    grad_out = cotangent.reshape(local_rows, channel_count)
    point_terms = jnp.dot(hid.T, grad_out, preferred_element_type=jnp.float32)
    grad_hid = jnp.dot(grad_out, w_point.T, preferred_element_type=jnp.float32)
    preactivation_gradient = gelu_back(pre, grad_hid).astype(jnp.bfloat16)
    dilated_terms = jnp.stack(
        [
            jnp.dot(
                kernel_taps[kernel_tap_index].T,
                preactivation_gradient,
                preferred_element_type=jnp.float32,
            )
            for kernel_tap_index in range(3)
        ]
    )
    centre_term = jnp.dot(
        preactivation_gradient, w_dilated[1].T, preferred_element_type=jnp.float32
    )
    first_terms = jnp.dot(
        preactivation_gradient, w_dilated[0].T, preferred_element_type=jnp.float32
    )
    last_terms = jnp.dot(preactivation_gradient, w_dilated[2].T, preferred_element_type=jnp.float32)
    from_later = passed_along(first_terms.astype(jnp.bfloat16), "seq", -HOPS).astype(
        first_terms.dtype
    )
    from_earlier = passed_along(last_terms.astype(jnp.bfloat16), "seq", HOPS).astype(
        last_terms.dtype
    )
    grad_act = centre_term + from_later + from_earlier
    normalized_gradient = gelu_back(normalized_input, grad_act)
    gain_contributions = jnp.sum(normalized_gradient * standardized_input, axis=0).reshape(
        1, channel_count
    )
    input_gradient = normalized_gradient * layer_norm_gain
    norm_part = inverse_deviation * (
        input_gradient
        - jnp.mean(input_gradient, axis=-1, keepdims=True)
        - standardized_input * jnp.mean(input_gradient * standardized_input, axis=-1, keepdims=True)
    )
    grad_inputs = (grad_out.astype(jnp.float32) + norm_part).astype(jnp.bfloat16)
    summed = (
        lax.psum_scatter(dilated_terms, "seq", scatter_dimension=1, tiled=True),
        lax.psum_scatter(point_terms, "seq", scatter_dimension=1, tiled=True),
        lax.psum_scatter(gain_contributions, "seq", scatter_dimension=1, tiled=True),
    )
    scale = lax.rsqrt(jnp.float32(row_total_count))
    return (
        outputs.reshape(num_seqs, local_bins, channel_count),
        grad_inputs.reshape(num_seqs, local_bins, channel_count),
        summed[0] * scale,
        summed[1] * scale,
        summed[2].reshape(-1) * scale,
    )


def solution(mesh):
    in_specs = (P("groups", "seq", None), P(), P(), P(), P("groups", "seq", None))
    out_specs = (
        P("groups", "seq", None),
        P("groups", "seq", None),
        P("groups", "seq", None),
        P("groups", "seq"),
        P(("groups", "seq")),
    )
    return jax.shard_map(
        per_device, mesh=mesh, in_specs=in_specs, out_specs=out_specs, check_vma=False
    )
```

profile of v0, /device:TPU:0, one launch (start us, length us, event | category | flops | bytes accessed | tf_op | source)
XLA Modules:
  0.0 370.0 jit_solution(14978041999356758671)
XLA Ops:
  7.2 1.8 convert_reduce_fusion
  9.1 0.6 fusion.16
  9.8 1.7 fusion.27
  11.5 6.0 %collective-permute-start = (bf16[1024,768]{1,0:T(8,128)(2,1)S(1)}, bf16[1024,768]{1,0:T(8,128)(2,1)S(1)}, u32[]{:S(2)}, u32[]{:S(2)}) collective-permute-start(bf16[1024,768]{1,0:T(8,128)(2,1)S(1)} %fusion.27), channel_id=1, source_target_pairs={{0,8},{1,9},{2,10},{3,11},{4,12},{5,13},{6,14},{7,15},{16,24},{17,... | collective-permute-start | bytes 4718600 | tf_op jit(solution)/shard_map/ppermute | solution.py:12
  17.5 1.3 collective-permute-start.1
  18.8 1.6 fusion.13
  20.5 1.0 fusion.49
  21.9 1.0 fusion.62
  22.9 28.3 %collective-permute-done = bf16[1024,768]{1,0:T(8,128)(2,1)S(1)} collective-permute-done((bf16[1024,768]{1,0:T(8,128)(2,1)S(1)}, bf16[1024,768]{1,0:T(8,128)(2,1)S(1)}, u32[]{:S(2)}, u32[]{:S(2)}) %collective-permute-start) | collective-permute-done | bytes 1572896 | tf_op jit(solution)/shard_map/ppermute | solution.py:12
  51.1 1.0 fusion.45
  52.3 37.6 %collective-permute-done.1 = bf16[1024,768]{1,0:T(8,128)(2,1)S(1)} collective-permute-done((bf16[1024,768]{1,0:T(8,128)(2,1)S(1)}, bf16[1024,768]{1,0:T(8,128)(2,1)S(1)}, u32[]{:S(2)}, u32[]{:S(2)}) %collective-permute-start.1) | collective-permute-done | bytes 1572896 | tf_op jit(solution)/shard_map/ppermute | solution.py:12
  89.9 3.1 fusion.41
  93.0 1.0 convolution_convert_fusion
  94.0 1.0 convolution_convert_fusion.1
  95.0 1.3 collective-permute-start.2
  96.3 5.6 %collective-permute-start.3 = (bf16[1024,768]{1,0:T(8,128)(2,1)S(1)}, bf16[1024,768]{1,0:T(8,128)(2,1)S(1)}, u32[]{:S(2)}, u32[]{:S(2)}) collective-permute-start(bf16[1024,768]{1,0:T(8,128)(2,1)S(1)} %convolution_convert_fusion), channel_id=1, source_target_pairs={{0,8},{1,9},{2,10},{3,11},{4,12},{5,13},{6,14},{7,15},{16,24},{17,... | collective-permute-start | bytes 4718600 | tf_op jit(solution)/shard_map/ppermute | solution.py:12
  101.9 62.9 %collective-permute-done.2 = bf16[1024,768]{1,0:T(8,128)(2,1)S(1)} collective-permute-done((bf16[1024,768]{1,0:T(8,128)(2,1)S(1)}, bf16[1024,768]{1,0:T(8,128)(2,1)S(1)}, u32[]{:S(2)}, u32[]{:S(2)}) %collective-permute-start.2) | collective-permute-done | bytes 1572896 | tf_op jit(solution)/shard_map/ppermute | solution.py:12
  164.9 5.4 %fusion.33 = (f32[768]{0:T(1024)S(1)}, f32[1024]{0:T(1024)S(1)}, f32[1024]{0:T(1024)S(1)}, f32[1024,768]{1,0:T(8,128)}) fusion(bf16[2,512,768]{2,1,0:T(8,128)(2,1)S(1)} %copy-done.1, f32[1024]{0:T(1024)S(1)} %bitcast.115, f32[1024]{0:T(1024)S(1)} %bitcast.112, f32[768]{0:T(1024)S(1)} %copy-done.6, bf16[1024,768]{1,0:T(8,128)(2,1)S(1)} %collective-permute-done.3, ...), kind=kOutput, calls=%fused_computation.41 | convolution fusion | flops 629929216 | bytes 9264128 | tf_op jit(solution)/shard_map/dot_general | solution.py:59
  170.2 0.9 reshape_bitcast_fusion
  171.4 4.0 %fusion.61 = f32[384,768]{0,1:T(8,128)} fusion(bf16[1024,768]{1,0:T(8,128)(2,1)} %bitcast.107, f32[1024,384]{1,0:T(8,128)} %get-tuple-element.13), kind=kOutput, calls=%fused_computation.85 | convolution fusion | flops 607518720 | bytes 4325376 | tf_op jit(solution)/shard_map/dot_general | solution.py:46
  175.5 2.5 convolution_bitcast_fusion.1
  178.0 1.0 convolution_bitcast_fusion
  179.5 1.0 convolution_bitcast_fusion.2
  180.5 2.0 pad_maximum_fusion
  182.5 4.0 %fusion.34 = bf16[1024,768]{1,0:T(8,128)(2,1)} fusion(bf16[2,512,768]{2,1,0:T(8,128)(2,1)S(1)} %copy-done.1, bf16[384,768]{1,0:T(8,128)(2,1)S(1)} %copy-done, f32[1024,384]{1,0:T(8,128)} %get-tuple-element.13), kind=kOutput, calls=%fused_computation.42 | convolution fusion | flops 609878016 | bytes 5308416 | tf_op jit(solution)/shard_map/dot_general | solution.py:42
  186.5 2.4 fusion.32
  188.9 40.3 %reduce-scatter.10.cloned.1.call-done = f32[48,1]{1,0:T(8,128)} async-done(((f32[768,1]{1,0:T(8,128)}), f32[48,1]{1,0:T(8,128)}) %reduce-scatter.10.cloned.1.call-update) | async-done | bytes 208
  229.2 0.7 multiply_bitcast_fusion
  230.5 59.9 %reduce-scatter.8.cloned.1.call-done = f32[384,48]{0,1:T(8,128)} async-done(((f32[384,768]{0,1:T(8,128)}), f32[384,48]{0,1:T(8,128)}) %reduce-scatter.8.cloned.1.call-update) | async-done | bytes 73744 | tf_op jit(solution)/shard_map/reduce_scatter | solution.py:86
  290.4 1.5 broadcast_multiply_fusion.1
  291.9 69.9 %reduce-scatter.6.cloned.1.call-done = f32[3,48,384]{2,1,0:T(8,128)} async-done(((f32[3,768,384]{2,1,0:T(8,128)}), f32[3,48,384]{2,1,0:T(8,128)}) %reduce-scatter.6.cloned.1.call-update) | async-done | bytes 221200 | tf_op jit(solution)/shard_map/reduce_scatter | solution.py:85
  361.8 1.6 broadcast_multiply_fusion
  (37 shorter events, 2.0 us)
Async XLA Ops:
  7.2 14.3 %copy-start = (bf16[384,768]{1,0:T(8,128)(2,1)S(1)}, bf16[384,768]{1,0:T(8,128)(2,1)}, u32[]{:S(2)}) copy-start(bf16[384,768]{1,0:T(8,128)(2,1)} %param.8) | copy-start | bytes 1769476
  7.2 1.9 copy-start.1
  7.2 2.6 copy-start.6
  7.2 222.0 %reduce-scatter.10.cloned.1.call-start = ((), (), s32[]{:S(2)}) async-start(), calls=%async_computation.5 | async-start | bytes 417792
  11.5 9.0 %copy-start.5 = (bf16[1024,768]{1,0:T(8,128)(2,1)}, bf16[1024,768]{1,0:T(8,128)(2,1)S(1)}, u32[]{:S(2)}) copy-start(bf16[1024,768]{1,0:T(8,128)(2,1)S(1)} %fusion.27) | copy-start | bytes 4718596
  11.5 39.6 %collective-permute-start = (bf16[1024,768]{1,0:T(8,128)(2,1)S(1)}, bf16[1024,768]{1,0:T(8,128)(2,1)S(1)}, u32[]{:S(2)}, u32[]{:S(2)}) collective-permute-start(bf16[1024,768]{1,0:T(8,128)(2,1)S(1)} %fusion.27), channel_id=1, source_target_pairs={{0,8},{1,9},{2,10},{3,11},{4,12},{5,13},{6,14},{7,15},{16,24},{17,... | collective-permute-start | bytes 4718600 | tf_op jit(solution)/shard_map/ppermute | solution.py:12
  17.5 72.4 %collective-permute-start.1 = (bf16[1024,768]{1,0:T(8,128)(2,1)S(1)}, bf16[1024,768]{1,0:T(8,128)(2,1)S(1)}, u32[]{:S(2)}, u32[]{:S(2)}) collective-permute-start(bf16[1024,768]{1,0:T(8,128)(2,1)S(1)} %fusion.27), channel_id=1, source_target_pairs={{8,0},{9,1},{10,2},{11,3},{12,4},{13,5},{14,6},{15,7},{24,16},{25,... | collective-permute-start | bytes 4718600 | tf_op jit(solution)/shard_map/ppermute | solution.py:12
  18.8 1.6 copy-start.7
  20.5 1.4 copy-start.2
  51.1 1.2 copy-start.8
  89.9 3.1 copy-start.10
  95.0 69.9 %collective-permute-start.2 = (bf16[1024,768]{1,0:T(8,128)(2,1)S(1)}, bf16[1024,768]{1,0:T(8,128)(2,1)S(1)}, u32[]{:S(2)}, u32[]{:S(2)}) collective-permute-start(bf16[1024,768]{1,0:T(8,128)(2,1)S(1)} %convolution_convert_fusion.1), channel_id=1, source_target_pairs={{8,0},{9,1},{10,2},{11,3},{12,4},{13,5},{14,6},{15,7},{24,16},{25,... | collective-permute-start | bytes 4718600 | tf_op jit(solution)/shard_map/ppermute | solution.py:12
  96.3 68.6 %collective-permute-start.3 = (bf16[1024,768]{1,0:T(8,128)(2,1)S(1)}, bf16[1024,768]{1,0:T(8,128)(2,1)S(1)}, u32[]{:S(2)}, u32[]{:S(2)}) collective-permute-start(bf16[1024,768]{1,0:T(8,128)(2,1)S(1)} %convolution_convert_fusion), channel_id=1, source_target_pairs={{0,8},{1,9},{2,10},{3,11},{4,12},{5,13},{6,14},{7,15},{16,24},{17,... | collective-permute-start | bytes 4718600 | tf_op jit(solution)/shard_map/ppermute | solution.py:12
  171.2 119.2 %reduce-scatter.8.cloned.1.call-start = ((), (), s32[]{:S(2)}) async-start(), calls=%async_computation.4 | async-start | bytes 1253376 | tf_op jit(solution)/shard_map/reduce_scatter | solution.py:86
  175.4 186.4 %reduce-scatter.6.cloned.1.call-start = ((), (), s32[]{:S(2)}) async-start(), calls=%async_computation.3 | async-start | bytes 3760128 | tf_op jit(solution)/shard_map/reduce_scatter | solution.py:85
  175.5 2.6 copy-start.11
  178.0 1.4 copy-start.9
  182.5 4.0 %copy-start.3 = (bf16[2,512,768]{2,1,0:T(8,128)(2,1)S(1)}, bf16[2,512,768]{2,1,0:T(8,128)(2,1)}, u32[]{:S(2)}) copy-start(bf16[2,512,768]{2,1,0:T(8,128)(2,1)} %param.9) | copy-start | bytes 4718596
  182.5 4.0 %copy-start.4 = (f32[1024,768]{1,0:T(8,128)S(1)}, f32[1024,768]{1,0:T(8,128)}, u32[]{:S(2)}) copy-start(f32[1024,768]{1,0:T(8,128)} %get-tuple-element.14) | copy-start | bytes 9437188
Sparse Core Ops, SparseCore 0:
  171.3 57.8 reduce-scatter.9
  233.3 57.0 reduce-scatter.7
  294.8 66.9 reduce-scatter.5
where the time goes:
time: 370 us
  waiting for transfers between devices  299 us (81%)
  matrix products  25.9 us (7%)
  starting transfers between devices  14.6 us (4%)
  other arithmetic  14 us (4%)
  between operations  14 us (4%)
    ppermute x4, waiting for transfers between devices, passed_along(): lax.ppermute(value, axis, [(source, source + steps) for source in range(l...  129 us
    reduce_scatter x1, waiting for transfers between devices, per_device(): lax.psum_scatter(dilated_terms, 'seq', scatter_dimension=1, tiled=True)  69.9 us
    reduce_scatter x1, waiting for transfers between devices, per_device(): lax.psum_scatter(point_terms, 'seq', scatter_dimension=1, tiled=True)  59.9 us
    unnamed x4, waiting for transfers between devices  40.3 us
    ppermute x4, starting transfers between devices, passed_along(): lax.ppermute(value, axis, [(source, source + steps) for source in range(l...  14.3 us
  transfers between devices with their start and end apart: 7, of which 6 were waited for; matrix products, arithmetic and copies ran while one was open for 7% of the time, Pallas kernels for 0%

commit v1 on v0

v1 whole, which is shorter than its diff:
```python
import jax
import jax.numpy as jnp
from jax import lax
from jax.sharding import PartitionSpec as P

DILATION = 4096
F32, BF16 = jnp.float32, jnp.bfloat16


def gelu_fn(value):
    return jax.nn.gelu(value, approximate=True)


def gelu_back(value, upstream):
    return jax.vjp(gelu_fn, value)[1](upstream)[0]


def dot(a, b):
    return jnp.dot(a, b, preferred_element_type=F32)


def dot_rows(a, b):
    return lax.dot_general(a, b, (((0,), (0,)), ((), ())), preferred_element_type=F32)


def dot_last(a, b):
    return lax.dot_general(a, b, (((1,), (1,)), ((), ())), preferred_element_type=F32)


def swap(value, bit):
    n = lax.axis_size("seq")
    return lax.ppermute(value, "seq", [(s, s ^ bit) for s in range(n)])


def shifted(value, steps):
    n = lax.axis_size("seq")
    return lax.ppermute(
        value, "seq", [(s, s + steps) for s in range(max(0, -steps), min(n, n - steps))]
    )


def halves(blocks, bit):
    pairs = blocks.reshape(blocks.shape[0] // 2, 2, *blocks.shape[1:])
    mine = (lax.axis_index("seq") & bit) != 0
    keep = jnp.where(mine, pairs[:, 1], pairs[:, 0])
    send = jnp.where(mine, pairs[:, 0], pairs[:, 1])
    return keep, send.astype(BF16)


def reduced(blocks, last=True):
    n = lax.axis_size("seq")
    bit = 1
    while bit < (n if last else n // 2):
        keep, send = halves(blocks, bit)
        blocks = keep + swap(send, bit).astype(F32)
        bit *= 2
    return blocks


def per_device(inputs, gain, w_dilated, w_point, cotangent):
    num_seqs, bins, channels = inputs.shape
    narrow = w_point.shape[0]
    n = lax.axis_size("seq")
    hops = DILATION // bins
    paired = n == 2 * hops
    rows_total = num_seqs * bins * n
    scale = lax.rsqrt(F32(rows_total))
    shard = channels // n
    upper = lax.axis_index("seq") >= hops

    if paired:
        w_far = jnp.where(upper, w_dilated[2], w_dilated[0])
        w_all = jnp.concatenate([w_far, w_dilated[1]], axis=1)
    else:
        w_all = jnp.concatenate([w_dilated[0], w_dilated[2], w_dilated[1]], axis=1)

    def exchange(value):
        if paired:
            return [swap(value[0], hops)]
        return [shifted(value[0], hops), shifted(value[-1], -hops)]

    def normalize(b):
        x = inputs[b].astype(F32)
        mid = x - jnp.mean(x, axis=-1, keepdims=True)
        inv = lax.rsqrt(jnp.mean(mid * mid, axis=-1, keepdims=True) + 1e-05)
        return x, mid * inv, inv

    acts, own, sent = [], [], []
    for b in range(num_seqs):
        _, xhat, _ = normalize(b)
        act = gelu_fn(xhat * gain).astype(BF16)
        acts.append(act)
        product = dot(act, w_all)
        far = product[:, :-narrow].astype(BF16)
        own.append(product[:, -narrow:])
        sent.append(exchange([far[:, :narrow], far[:, -narrow:]]))

    outs, hids, grads_pre, arrived = [], [], [], []
    for b in range(num_seqs):
        grad_hid = dot_last(cotangent[b], w_point)
        pre = own[b]
        for term in sent[b]:
            pre = pre + term.astype(F32)
        hid = gelu_fn(pre).astype(BF16)
        grad_pre = gelu_back(pre, grad_hid).astype(BF16)
        arrived.append(exchange([grad_pre, grad_pre]))
        hids.append(hid)
        grads_pre.append(grad_pre)
        outs.append((inputs[b].astype(F32) + dot(hid, w_point)).astype(BF16))
    outputs = jnp.stack(outs)

    act_all = jnp.concatenate(acts)
    point_terms = dot_rows(cotangent.reshape(-1, channels), jnp.concatenate(hids))
    centre_terms = dot_rows(act_all, jnp.concatenate(grads_pre))
    early = jnp.concatenate(
        [centre_terms.reshape(n, shard, narrow), point_terms.reshape(n, shard, narrow)], axis=1
    )
    early = reduced(early)[0] * scale

    grad_in, gain_terms = [], jnp.zeros((channels,), F32)
    for b in range(num_seqs):
        _, xhat, inv = normalize(b)
        normed = xhat * gain
        if paired:
            back = jnp.concatenate([arrived[b][0], grads_pre[b]], axis=1)
        else:
            back = jnp.concatenate([arrived[b][1], arrived[b][0], grads_pre[b]], axis=1)
        grad_act = dot_last(back, w_all)
        grad_normed = gelu_back(normed, grad_act)
        gain_terms = gain_terms + jnp.sum(grad_normed * xhat, axis=0)
        gx = grad_normed * gain
        part = inv * (
            gx
            - jnp.mean(gx, axis=-1, keepdims=True)
            - xhat * jnp.mean(gx * xhat, axis=-1, keepdims=True)
        )
        grad_in.append((cotangent[b].astype(F32) + part).astype(BF16))
    grad_inputs = jnp.stack(grad_in)

    gain_block = jnp.pad(gain_terms.reshape(n, 1, shard), ((0, 0), (0, 15), (0, narrow - shard)))
    if paired:
        far_terms = dot_rows(act_all, jnp.concatenate([a[0] for a in arrived]))
        late = jnp.concatenate([far_terms.reshape(n, shard, narrow), gain_block], axis=1)
        late = reduced(late, last=False)
        keep, send = halves(late, n // 2)
        keep, other = keep[0], swap(send, n // 2)[0].astype(F32)
        first = jnp.where(upper, other[:shard], keep[:shard])
        final = jnp.where(upper, keep[:shard], other[:shard])
        gain_sum = keep[shard, :shard] + other[shard, :shard]
    else:
        zero_terms = dot_rows(act_all, jnp.concatenate([a[1] for a in arrived]))
        two_terms = dot_rows(act_all, jnp.concatenate([a[0] for a in arrived]))
        late = jnp.concatenate(
            [zero_terms.reshape(n, shard, narrow), two_terms.reshape(n, shard, narrow), gain_block],
            axis=1,
        )
        late = reduced(late)[0]
        first, final = late[:shard], late[shard : 2 * shard]
        gain_sum = late[2 * shard, :shard]
    grad_dilated = jnp.stack([first * scale, early[:shard], final * scale])
    return outputs, grad_inputs, grad_dilated, early[shard:].T, gain_sum * scale


def solution(mesh):
    in_specs = (P("groups", "seq", None), P(), P(), P(), P("groups", "seq", None))
    out_specs = (
        P("groups", "seq", None),
        P("groups", "seq", None),
        P("groups", "seq", None),
        P("groups", "seq"),
        P(("groups", "seq")),
    )
    return jax.shard_map(
        per_device, mesh=mesh, in_specs=in_specs, out_specs=out_specs, check_vma=False
    )
```

time: 370 us -> 123 us (0.33)
  waiting for transfers between devices: 299 us -> 55.2 us
  between operations: 14 us -> 1.06 us
  local copies, waits for them, and re-layouts: 2.6 us -> 7.57 us
    reduce_scatter x2 -> x0, waiting for transfers between devices: 130 us -> none  [the longest x1 69.9 us: per_device(): lax.psum_scatter(dilated_terms, 'seq', scatter_dimension=1, tiled=True)]
    ppermute x4 -> x12, waiting for transfers between devices: 129 us -> 55.2 us  [swap(): return lax.ppermute(value, 'seq', [(s, s ^ bit) for s in range(n)])]
    unnamed x4 -> x0, waiting for transfers between devices: 40.3 us -> none
    ppermute x4 -> x12, starting transfers between devices: 14.3 us -> 15.6 us  [swap(): return lax.ppermute(value, 'seq', [(s, s ^ bit) for s in range(n)])]
    dot_general x12 -> x11, matrix products: 25.9 us -> 25.4 us  [the longest x4 14 us: dot_last(): lax.dot_general(a, b, (((1,), (1,)), ((), ())), preferred_element_type=F32)]
  transfers between devices with their start and end apart: 7 -> 12, of which waited for: 6 -> 7; matrix products, arithmetic and copies ran while one was open for 7% -> 31% of each run, Pallas kernels for 0% -> 0%
where the time goes in v1:
time: 123 us; the launch traced here: 122 us
  waiting for transfers between devices  55.2 us (45%)
  matrix products  25.4 us (21%)
  other arithmetic  17.5 us (14%)
  starting transfers between devices  15.6 us (13%)
  local copies, waits for them, and re-layouts  7.57 us (6%)
    ppermute x12, waiting for transfers between devices, swap(): return lax.ppermute(value, 'seq', [(s, s ^ bit) for s in range(n)])  55.2 us
    ppermute x12, starting transfers between devices, swap(): return lax.ppermute(value, 'seq', [(s, s ^ bit) for s in range(n)])  15.6 us
    dot_general x4, matrix products, dot_last(): lax.dot_general(a, b, (((1,), (1,)), ((), ())), preferred_element_type=F32)  14 us
    dot_general x3, matrix products, dot_rows(): lax.dot_general(a, b, (((0,), (0,)), ((), ())), preferred_element_type=F32)  7.84 us
    unnamed x46, local copies, waits for them, and re-layouts  4.25 us
    dot_general x4, matrix products, dot(): return jnp.dot(a, b, preferred_element_type=F32)  3.59 us
    another operation x2, other arithmetic, per_device(): grad_inputs = jnp.stack(grad_in)  2.66 us
    convert_element_type x2, other arithmetic, per_device(): hid = gelu_fn(pre).astype(BF16)  2.63 us
  transfers between devices with their start and end apart: 12, of which 7 were waited for; matrix products, arithmetic and copies ran while one was open for 31% of the time, Pallas kernels for 0%

profile of v1, /device:TPU:0, one launch (start us, length us, event | category | flops | bytes accessed | tf_op | source)
XLA Modules:
  0.0 122.3 jit_solution(3872434911770410982)
XLA Ops:
  0.7 1.8 %convert_reduce_fusion.1 = (f32[512]{0:T(512)S(1)}, f32[512]{0:T(512)S(1)}) fusion(bf16[2,512,768]{2,1,0:T(8,128)(2,1)} %param.5), kind=kLoop, calls=%fused_computation.10 | loop fusion | flops 1571840 | bytes 1576960 | tf_op jit(solution)/shard_map/reduce_sum | solution.py:84
  3.2 1.5 %select_bitcast_fusion = (bf16[768,384]{1,0:T(8,128)(2,1)S(1)}, bf16[768,384]{1,0:T(8,128)(2,1)S(1)}) fusion(bf16[3,768,384]{2,1,0:T(8,128)(2,1)} %param.7, pred[]{:T(512)S(6)} %ge.3), kind=kLoop, calls=%fused_computation.144 | loop fusion | flops 294912 | bytes 2949121 | tf_op jit(solution)/shard_map/jit(_where)/select_n | solution.py:72
  4.8 1.6 %fusion.36 = (bf16[512,768]{1,0:T(8,128)(2,1)S(1)}, bf16[512,768]{1,0:T(8,128)(2,1)S(1)}) fusion(f32[768]{0:T(1024)S(1)} %copy-done.22, f32[512]{0:T(512)S(1)} %add_rsqrt_fusion.1, f32[512]{0:T(512)S(1)} %get-tuple-element.33, bf16[2,512,768]{2,1,0:T(8,128)(2,1)S(1)} %copy-done.1, f32[512]{0:T(512)S(1)} %add_rsqrt_fusion, f32[512]{0:T(512)S(1)} %get-tuple-element.32), kind=kLoop, calls=%fused_computation.46 | loop fusion | flops 10223616 | bytes 3156992 | tf_op jit(solution)/shard_map/convert_element_type | solution.py:91
  8.1 4.0 %collective-permute-start = (bf16[512,384]{1,0:T(8,128)(2,1)}, bf16[512,384]{1,0:T(8,128)(2,1)}, u32[]{:S(2)}, u32[]{:S(2)}) collective-permute-start(bf16[512,384]{1,0:T(8,128)(2,1)} %slice.344), channel_id=1, source_target_pairs={{0,8},{1,9},{2,10},{3,11},{4,12},{5,13},{6,14},{7,15},{8,0},{9,1},... | collective-permute-start | bytes 1179656 | tf_op jit(solution)/shard_map/ppermute | solution.py:32
  13.0 1.1 copy-done.13
  14.1 25.1 %collective-permute-done = bf16[512,384]{1,0:T(8,128)(2,1)} collective-permute-done((bf16[512,384]{1,0:T(8,128)(2,1)}, bf16[512,384]{1,0:T(8,128)(2,1)}, u32[]{:S(2)}, u32[]{:S(2)}) %collective-permute-start) | collective-permute-done | bytes 393248 | tf_op jit(solution)/shard_map/ppermute | solution.py:32
  39.3 3.2 %fusion.67 = bf16[512,384]{1,0:T(8,128)(2,1)} fusion(bf16[384,768]{1,0:T(8,128)(2,1)S(1)} %copy-done, bf16[2,512,768]{2,1,0:T(8,128)(2,1)} %param.9, bf16[512,384]{1,0:T(8,128)(2,1)} %collective-permute-done, f32[512,768]{1,0:T(8,128)} %copy-done.11), kind=kOutput, calls=%fused_computation.93 | convolution fusion | flops 306315264 | bytes 2949120 | tf_op jit(solution)/shard_map/dot_general | solution.py:27
  42.5 13.6 %collective-permute-done.1 = bf16[512,384]{1,0:T(8,128)(2,1)} collective-permute-done((bf16[512,384]{1,0:T(8,128)(2,1)S(1)}, bf16[512,384]{1,0:T(8,128)(2,1)}, u32[]{:S(2)}, u32[]{:S(2)}) %collective-permute-start.1) | collective-permute-done | bytes 393248 | tf_op jit(solution)/shard_map/ppermute | solution.py:32
  56.1 2.7 %fusion.74 = bf16[512,384]{1,0:T(8,128)(2,1)} fusion(bf16[384,768]{1,0:T(8,128)(2,1)S(1)} %copy-done, bf16[2,512,768]{2,1,0:T(8,128)(2,1)S(1)} %copy-done.4, bf16[512,384]{1,0:T(8,128)(2,1)} %collective-permute-done.1, f32[512,768]{1,0:T(8,128)S(1)} %copy-done.14), kind=kOutput, calls=%fused_computation.100 | convolution fusion | flops 306315264 | bytes 2949120 | tf_op jit(solution)/shard_map/dot_general | solution.py:27
  58.9 3.3 %fusion.59 = f32[768,384]{1,0:T(8,128)} fusion(bf16[512,768]{1,0:T(8,128)(2,1)S(1)} %copy-done.17, bf16[512,768]{1,0:T(8,128)(2,1)S(1)} %get-tuple-element.21, bf16[512,384]{1,0:T(8,128)(2,1)} %fusion.74, bf16[512,384]{1,0:T(8,128)(2,1)} %fusion.67), kind=kOutput, calls=%fused_computation.85 | convolution fusion | flops 608698368 | bytes 3538944 | tf_op jit(solution)/shard_map/dot_general | solution.py:23
  62.1 1.3 %multiply_convert_fusion.1 = bf16[512,384]{1,0:T(8,128)(2,1)S(1)} fusion(bf16[512,384]{1,0:T(8,128)(2,1)} %collective-permute-done, f32[512,768]{1,0:T(8,128)S(1)} %copy-done.12), kind=kLoop, calls=%fused_computation.135 | loop fusion | flops 2162688 | bytes 1572864 | tf_op jit(solution)/shard_map/convert_element_type | solution.py:104
  63.5 1.5 %fusion.55 = bf16[1,512,768]{2,1,0:T(8,128)(2,1)} fusion(bf16[512,384]{1,0:T(8,128)(2,1)S(1)} %multiply_convert_fusion.1, bf16[384,768]{1,0:T(8,128)(2,1)S(1)} %copy-done, bf16[2,512,768]{2,1,0:T(8,128)(2,1)S(1)} %copy-done.1), kind=kOutput, calls=%fused_computation.73 | convolution fusion | flops 303169536 | bytes 2555904 | tf_op jit(solution)/shard_map/dot_general | solution.py:19
  64.9 1.3 %multiply_convert_fusion = bf16[512,384]{1,0:T(8,128)(2,1)S(1)} fusion(bf16[512,384]{1,0:T(8,128)(2,1)} %collective-permute-done.1, f32[512,768]{1,0:T(8,128)S(1)} %copy-done.14), kind=kLoop, calls=%fused_computation.134 | loop fusion | flops 2162688 | bytes 1572864 | tf_op jit(solution)/shard_map/convert_element_type | solution.py:104
  67.0 1.8 %convolution_bitcast_fusion = f32[768,384]{0,1:T(8,128)} fusion(bf16[1024,768]{1,0:T(8,128)(2,1)S(1)} %bitcast.350, bf16[512,384]{1,0:T(8,128)(2,1)S(1)} %multiply_convert_fusion, bf16[512,384]{1,0:T(8,128)(2,1)S(1)} %multiply_convert_fusion.1), kind=kOutput, calls=%fused_computation.69 | convolution fusion | flops 605552640 | bytes 3538944 | tf_op jit(solution)/shard_map/dot_general | solution.py:23
  68.8 1.6 %copy.72 = f32[768,384]{1,0:T(8,128)S(1)} copy(f32[768,384]{0,1:T(8,128)} %convolution_bitcast_fusion) | data formatting | bytes 2359296 | tf_op jit(solution)/shard_map/dot_general | solution.py:23
  70.5 2.2 %fusion.111 = bf16[8,96,384]{2,1,0:T(8,128)(2,1)} fusion(pred[]{:T(512)S(6)} %ne.19, f32[8,2,48,384]{3,2,1,0:T(8,128)S(1)} %bitcast.334, f32[8,2,48,384]{3,2,1,0:T(8,128)} %bitcast.340), kind=kLoop, calls=%fused_computation.138 | loop fusion | flops 2654208 | bytes 2949121 | tf_op jit(solution)/shard_map/convert_element_type | solution.py:47
  73.9 1.3 %pad_maximum_fusion = bf16[2,512,768]{2,1,0:T(8,128)(2,1)} fusion(bf16[1,512,768]{2,1,0:T(8,128)(2,1)S(1)} %fusion.54, bf16[1,512,768]{2,1,0:T(8,128)(2,1)S(1)} %copy-done.3), kind=kLoop, calls=%fused_computation.64 | loop fusion | flops 786432 | bytes 3145728 | tf_op jit(solution)/shard_map/stack | solution.py:110
  75.1 5.5 %collective-permute-done.3 = bf16[512,384]{1,0:T(8,128)(2,1)} collective-permute-done((bf16[512,384]{1,0:T(8,128)(2,1)}, bf16[512,384]{1,0:T(8,128)(2,1)}, u32[]{:S(2)}, u32[]{:S(2)}) %collective-permute-start.3) | collective-permute-done | bytes 393248 | tf_op jit(solution)/shard_map/ppermute | solution.py:32
  80.6 2.8 %fusion.53 = f32[512,768]{1,0:T(8,128)S(1)} fusion(bf16[512,384]{1,0:T(8,128)(2,1)} %fusion.74, bf16[512,384]{1,0:T(8,128)(2,1)} %collective-permute-done.3, f32[512]{0:T(512)S(1)} %add_rsqrt_fusion, f32[512]{0:T(512)S(1)} %get-tuple-element.32, f32[768]{0:T(1024)S(1)} %copy-done.22, bf16[2,512,768]{2,1,0:T(8,128)(2,1)S(1)} %copy-done.1, ...), kind=kOutput, calls=%fused_computation.63 | convolution fusion | flops 616955904 | bytes 4332544 | tf_op jit(solution)/shard_map/dot_general | solution.py:27
  83.4 5.3 %fusion.44 = (f32[768]{0:T(1024)S(1)}, f32[512]{0:T(512)S(1)}, f32[512]{0:T(512)S(1)}, f32[768]{0:T(1024)S(1)}, f32[512]{0:T(512)S(1)}, /*index=5*/f32[512]{0:T(512)S(1)}, f32[512,768]{1,0:T(8,128)}) fusion(f32[512]{0:T(512)S(1)} %add_rsqrt_fusion.1, f32[512]{0:T(512)S(1)} %get-tuple-element.33, bf16[2,512,768]{2,1,0:T(8,128)(2,1)S(1)} %copy-done.1, ...), kind=kOutput, calls=%fused_computation.54 | convolution fusion | flops 622850560 | bytes 6710272 | tf_op jit(solution)/shard_map/dot_general | solution.py:27
  88.9 2.7 %fusion.60 = f32[768,384]{1,0:T(8,128)S(1)} fusion(bf16[512,768]{1,0:T(8,128)(2,1)} %copy-done.16, bf16[512,768]{1,0:T(8,128)(2,1)} %copy-done.15, bf16[512,384]{1,0:T(8,128)(2,1)} %collective-permute-done.3, bf16[512,384]{1,0:T(8,128)(2,1)} %collective-permute-done.2), kind=kOutput, calls=%fused_computation.86 | convolution fusion | flops 608698368 | bytes 3538944 | tf_op jit(solution)/shard_map/dot_general | solution.py:23
  91.8 1.2 copy-done.5
  93.0 1.4 %fusion.77 = (bf16[1,512,768]{2,1,0:T(8,128)(2,1)S(1)}, bf16[1,512,768]{2,1,0:T(8,128)(2,1)S(1)}) fusion(f32[512,768]{1,0:T(8,128)S(1)} %copy-done.8, f32[512]{0:T(512)S(1)} %broadcast_multiply_fusion.2, f32[512]{0:T(512)S(1)} %broadcast_multiply_fusion.3, f32[768]{0:T(1024)S(1)} %copy-done.22, f32[512]{0:T(512)S(1)} %add_rsqrt_fusion.1, ...), kind=kLoop, calls=%fused_computation.103 | loop fusion | flops 8650752 | bytes 7883776 | tf_op jit(solution)/shard_map/stack | solution.py:138
  94.4 1.3 %pad_maximum_fusion.1 = bf16[2,512,768]{2,1,0:T(8,128)(2,1)} fusion(bf16[1,512,768]{2,1,0:T(8,128)(2,1)S(1)} %get-tuple-element.18, bf16[1,512,768]{2,1,0:T(8,128)(2,1)S(1)} %get-tuple-element.17), kind=kLoop, calls=%fused_computation.65 | loop fusion | flops 786432 | bytes 3145728 | tf_op jit(solution)/shard_map/stack | solution.py:138
  96.2 1.2 fusion.58
  97.4 1.7 %collective-permute-start.9 = (bf16[4,96,384]{2,1,0:T(8,128)(2,1)S(1)}, bf16[4,96,384]{2,1,0:T(8,128)(2,1)S(1)}, u32[]{:S(2)}, u32[]{:S(2)}) collective-permute-start(bf16[4,96,384]{2,1,0:T(8,128)(2,1)S(1)} %fusion.115), channel_id=1, source_target_pairs={{0,2},{1,3},{2,0},{3,1},{4,6},{5,7},{6,4},{7,5},{8,10},{9,11},{10,... | collective-permute-start | bytes 884744 | tf_op jit(solution)/shard_map/ppermute | solution.py:32
  99.8 7.7 %collective-permute-done.9 = bf16[4,96,384]{2,1,0:T(8,128)(2,1)S(1)} collective-permute-done((bf16[4,96,384]{2,1,0:T(8,128)(2,1)S(1)}, bf16[4,96,384]{2,1,0:T(8,128)(2,1)S(1)}, u32[]{:S(2)}, u32[]{:S(2)}) %collective-permute-start.9) | collective-permute-done | bytes 294944 | tf_op jit(solution)/shard_map/ppermute | solution.py:32
  107.6 2.5 %collective-permute-start.10 = (bf16[2,96,384]{2,1,0:T(8,128)(2,1)S(1)}, bf16[2,96,384]{2,1,0:T(8,128)(2,1)S(1)}, u32[]{:S(2)}, u32[]{:S(2)}) collective-permute-start(bf16[2,96,384]{2,1,0:T(8,128)(2,1)S(1)} %fusion.121), channel_id=1, source_target_pairs={{0,4},{1,5},{2,6},{3,7},{4,0},{5,1},{6,2},{7,3},{8,12},{9,13},{10,... | collective-permute-start | bytes 442376 | tf_op jit(solution)/shard_map/ppermute | solution.py:32
  110.2 3.0 %collective-permute-start.6 = (bf16[2,64,384]{2,1,0:T(8,128)(2,1)S(1)}, bf16[2,64,384]{2,1,0:T(8,128)(2,1)S(1)}, u32[]{:S(2)}, u32[]{:S(2)}) collective-permute-start(bf16[2,64,384]{2,1,0:T(8,128)(2,1)S(1)} %fusion.123), channel_id=1, source_target_pairs={{0,4},{1,5},{2,6},{3,7},{4,0},{5,1},{6,2},{7,3},{8,12},{9,13},{10,... | collective-permute-start | bytes 294920 | tf_op jit(solution)/shard_map/ppermute | solution.py:32
  113.3 1.8 %collective-permute-start.11 = (bf16[1,96,384]{2,1,0:T(8,128)(2,1)S(1)}, bf16[1,96,384]{2,1,0:T(8,128)(2,1)S(1)}, u32[]{:S(2)}, u32[]{:S(2)}) collective-permute-start(bf16[1,96,384]{2,1,0:T(8,128)(2,1)S(1)} %fusion.124), channel_id=1, source_target_pairs={{0,8},{1,9},{2,10},{3,11},{4,12},{5,13},{6,14},{7,15},{8,0},{9,1},... | collective-permute-start | bytes 221192 | tf_op jit(solution)/shard_map/ppermute | solution.py:32
  116.0 2.0 %collective-permute-start.7 = (bf16[1,64,384]{2,1,0:T(8,128)(2,1)S(1)}, bf16[1,64,384]{2,1,0:T(8,128)(2,1)S(1)}, u32[]{:S(2)}, u32[]{:S(2)}) collective-permute-start(bf16[1,64,384]{2,1,0:T(8,128)(2,1)S(1)} %fusion.125), channel_id=1, source_target_pairs={{0,8},{1,9},{2,10},{3,11},{4,12},{5,13},{6,14},{7,15},{8,0},{9,1},... | collective-permute-start | bytes 147464 | tf_op jit(solution)/shard_map/ppermute | solution.py:32
  119.7 1.3 %collective-permute-done.7 = bf16[1,64,384]{2,1,0:T(8,128)(2,1)S(1)} collective-permute-done((bf16[1,64,384]{2,1,0:T(8,128)(2,1)S(1)}, bf16[1,64,384]{2,1,0:T(8,128)(2,1)S(1)}, u32[]{:S(2)}, u32[]{:S(2)}) %collective-permute-start.7) | collective-permute-done | bytes 49184 | tf_op jit(solution)/shard_map/ppermute | solution.py:32
  (92 shorter events, 10.7 us)
Async XLA Ops:
  0.6 38.7 %copy-start = (bf16[384,768]{1,0:T(8,128)(2,1)S(1)}, bf16[384,768]{1,0:T(8,128)(2,1)}, u32[]{:S(2)}) copy-start(bf16[384,768]{1,0:T(8,128)(2,1)} %param.8) | copy-start | bytes 1769476
  0.6 1.9 %copy-start.1 = (bf16[2,512,768]{2,1,0:T(8,128)(2,1)S(1)}, bf16[2,512,768]{2,1,0:T(8,128)(2,1)}, u32[]{:S(2)}) copy-start(bf16[2,512,768]{2,1,0:T(8,128)(2,1)} %param.5) | copy-start | bytes 4718596
  3.2 1.6 %copy-start.22 = (f32[768]{0:T(1024)S(1)}, f32[768]{0:T(1024)}, u32[]{:S(2)}) copy-start(f32[768]{0:T(1024)} %param.6) | copy-start | bytes 9220
  4.8 7.4 %copy-start.18 = (bf16[768,384]{1,0:T(8,128)(2,1)}, bf16[768,384]{1,0:T(8,128)(2,1)S(1)}, u32[]{:S(2)}) copy-start(bf16[768,384]{1,0:T(8,128)(2,1)S(1)} %get-tuple-element.19) | copy-start | bytes 1769476
  4.8 7.4 %copy-start.20 = (bf16[768,384]{1,0:T(8,128)(2,1)}, bf16[768,384]{1,0:T(8,128)(2,1)S(1)}, u32[]{:S(2)}) copy-start(bf16[768,384]{1,0:T(8,128)(2,1)S(1)} %get-tuple-element.20) | copy-start | bytes 1769476
  6.4 5.7 %copy-start.16 = (bf16[512,768]{1,0:T(8,128)(2,1)}, bf16[512,768]{1,0:T(8,128)(2,1)S(1)}, u32[]{:S(2)}) copy-start(bf16[512,768]{1,0:T(8,128)(2,1)S(1)} %get-tuple-element.22) | copy-start | bytes 2359300
  6.5 52.4 %copy-start.15 = (bf16[512,768]{1,0:T(8,128)(2,1)}, bf16[512,768]{1,0:T(8,128)(2,1)S(1)}, u32[]{:S(2)}) copy-start(bf16[512,768]{1,0:T(8,128)(2,1)S(1)} %get-tuple-element.21) | copy-start | bytes 2359300
  7.2 5.7 %copy-start.11 = (f32[512,768]{1,0:T(8,128)}, f32[512,768]{1,0:T(8,128)S(1)}, u32[]{:S(2)}) copy-start(f32[512,768]{1,0:T(8,128)S(1)} %fusion.136) | copy-start | bytes 4718596
  8.1 31.1 %collective-permute-start = (bf16[512,384]{1,0:T(8,128)(2,1)}, bf16[512,384]{1,0:T(8,128)(2,1)}, u32[]{:S(2)}, u32[]{:S(2)}) collective-permute-start(bf16[512,384]{1,0:T(8,128)(2,1)} %slice.344), channel_id=1, source_target_pairs={{0,8},{1,9},{2,10},{3,11},{4,12},{5,13},{6,14},{7,15},{8,0},{9,1},... | collective-permute-start | bytes 1179656 | tf_op jit(solution)/shard_map/ppermute | solution.py:32
  14.1 42.0 %collective-permute-start.1 = (bf16[512,384]{1,0:T(8,128)(2,1)S(1)}, bf16[512,384]{1,0:T(8,128)(2,1)}, u32[]{:S(2)}, u32[]{:S(2)}) collective-permute-start(bf16[512,384]{1,0:T(8,128)(2,1)S(1)} %slice.343), channel_id=1, source_target_pairs={{0,8},{1,9},{2,10},{3,11},{4,12},{5,13},{6,14},{7,15},{8,0},{9,1},... | collective-permute-start | bytes 1179656 | tf_op jit(solution)/shard_map/ppermute | solution.py:32
  14.1 42.0 %copy-start.4 = (bf16[2,512,768]{2,1,0:T(8,128)(2,1)S(1)}, bf16[2,512,768]{2,1,0:T(8,128)(2,1)}, u32[]{:S(2)}) copy-start(bf16[2,512,768]{2,1,0:T(8,128)(2,1)} %param.9) | copy-start | bytes 4718596
  14.1 42.0 %copy-start.14 = (f32[512,768]{1,0:T(8,128)S(1)}, f32[512,768]{1,0:T(8,128)}, u32[]{:S(2)}) copy-start(f32[512,768]{1,0:T(8,128)} %copy-done.13) | copy-start | bytes 4718596
  42.5 16.4 %copy-start.17 = (bf16[512,768]{1,0:T(8,128)(2,1)S(1)}, bf16[512,768]{1,0:T(8,128)(2,1)}, u32[]{:S(2)}) copy-start(bf16[512,768]{1,0:T(8,128)(2,1)} %copy-done.16) | copy-start | bytes 2359300
  42.5 40.9 %collective-permute-start.2 = (bf16[512,384]{1,0:T(8,128)(2,1)}, bf16[512,384]{1,0:T(8,128)(2,1)}, u32[]{:S(2)}, u32[]{:S(2)}) collective-permute-start(bf16[512,384]{1,0:T(8,128)(2,1)} %fusion.67), channel_id=1, source_target_pairs={{0,8},{1,9},{2,10},{3,11},{4,12},{5,13},{6,14},{7,15},{8,0},{9,1},... | collective-permute-start | bytes 1179656 | tf_op jit(solution)/shard_map/ppermute | solution.py:32
  58.9 3.3 %copy-start.12 = (f32[512,768]{1,0:T(8,128)S(1)}, f32[512,768]{1,0:T(8,128)}, u32[]{:S(2)}) copy-start(f32[512,768]{1,0:T(8,128)} %copy-done.11) | copy-start | bytes 4718596
  58.9 21.7 %collective-permute-start.3 = (bf16[512,384]{1,0:T(8,128)(2,1)}, bf16[512,384]{1,0:T(8,128)(2,1)}, u32[]{:S(2)}, u32[]{:S(2)}) collective-permute-start(bf16[512,384]{1,0:T(8,128)(2,1)} %fusion.74), channel_id=1, source_target_pairs={{0,8},{1,9},{2,10},{3,11},{4,12},{5,13},{6,14},{7,15},{8,0},{9,1},... | collective-permute-start | bytes 1179656 | tf_op jit(solution)/shard_map/ppermute | solution.py:32
  70.5 2.3 %copy-start.10 = (bf16[512,384]{1,0:T(8,128)(2,1)S(1)}, bf16[512,384]{1,0:T(8,128)(2,1)}, u32[]{:S(2)}) copy-start(bf16[512,384]{1,0:T(8,128)(2,1)} %copy-done.9) | copy-start | bytes 1179652
  72.7 23.0 %collective-permute-start.8 = (bf16[8,96,384]{2,1,0:T(8,128)(2,1)}, bf16[8,96,384]{2,1,0:T(8,128)(2,1)}, u32[]{:S(2)}, u32[]{:S(2)}) collective-permute-start(bf16[8,96,384]{2,1,0:T(8,128)(2,1)} %fusion.111), channel_id=1, source_target_pairs={{0,1},{1,0},{2,3},{3,2},{4,5},{5,4},{6,7},{7,6},{8,9},{9,8},{10,11... | collective-permute-start | bytes 1769480 | tf_op jit(solution)/shard_map/ppermute | solution.py:32
  73.9 6.7 %copy-start.19 = (bf16[768,384]{1,0:T(8,128)(2,1)S(1)}, bf16[768,384]{1,0:T(8,128)(2,1)}, u32[]{:S(2)}) copy-start(bf16[768,384]{1,0:T(8,128)(2,1)} %copy-done.18) | copy-start | bytes 1769476
  73.9 6.7 %copy-start.21 = (bf16[768,384]{1,0:T(8,128)(2,1)S(1)}, bf16[768,384]{1,0:T(8,128)(2,1)}, u32[]{:S(2)}) copy-start(bf16[768,384]{1,0:T(8,128)(2,1)} %copy-done.20) | copy-start | bytes 1769476
  83.4 5.3 %copy-start.6 = (f32[512,768]{1,0:T(8,128)}, f32[512,768]{1,0:T(8,128)S(1)}, u32[]{:S(2)}) copy-start(f32[512,768]{1,0:T(8,128)S(1)} %fusion.53) | copy-start | bytes 4718596
  88.8 2.9 %copy-start.7 = (f32[512,768]{1,0:T(8,128)S(1)}, f32[512,768]{1,0:T(8,128)}, u32[]{:S(2)}) copy-start(f32[512,768]{1,0:T(8,128)} %copy-done.6) | copy-start | bytes 4718596
  88.9 2.9 %copy-start.8 = (f32[512,768]{1,0:T(8,128)S(1)}, f32[512,768]{1,0:T(8,128)}, u32[]{:S(2)}) copy-start(f32[512,768]{1,0:T(8,128)} %get-tuple-element.31) | copy-start | bytes 4718596
  91.6 1.4 %copy-start.5 = (bf16[2,512,768]{2,1,0:T(8,128)(2,1)S(1)}, bf16[2,512,768]{2,1,0:T(8,128)(2,1)}, u32[]{:S(2)}) copy-start(bf16[2,512,768]{2,1,0:T(8,128)(2,1)} %param.9) | copy-start | bytes 4718596
  91.7 7.4 %collective-permute-start.4 = (bf16[8,64,384]{2,1,0:T(8,128)(2,1)S(1)}, bf16[8,64,384]{2,1,0:T(8,128)(2,1)S(1)}, u32[]{:S(2)}, u32[]{:S(2)}) collective-permute-start(bf16[8,64,384]{2,1,0:T(8,128)(2,1)S(1)} %fusion.112), channel_id=1, source_target_pairs={{0,1},{1,0},{2,3},{3,2},{4,5},{5,4},{6,7},{7,6},{8,9},{9,8},{10,11... | collective-permute-start | bytes 1179656 | tf_op jit(solution)/shard_map/ppermute | solution.py:32
  94.4 1.7 %copy-start.2 = (f32[768,384]{1,0:T(8,128)S(1)}, f32[768,384]{1,0:T(8,128)}, u32[]{:S(2)}) copy-start(f32[768,384]{1,0:T(8,128)} %fusion.59) | copy-start | bytes 3538948
  97.4 10.0 %collective-permute-start.9 = (bf16[4,96,384]{2,1,0:T(8,128)(2,1)S(1)}, bf16[4,96,384]{2,1,0:T(8,128)(2,1)S(1)}, u32[]{:S(2)}, u32[]{:S(2)}) collective-permute-start(bf16[4,96,384]{2,1,0:T(8,128)(2,1)S(1)} %fusion.115), channel_id=1, source_target_pairs={{0,2},{1,3},{2,0},{3,1},{4,6},{5,7},{6,4},{7,5},{8,10},{9,11},{10,... | collective-permute-start | bytes 884744 | tf_op jit(solution)/shard_map/ppermute | solution.py:32
  99.3 10.8 %collective-permute-start.5 = (bf16[4,64,384]{2,1,0:T(8,128)(2,1)S(1)}, bf16[4,64,384]{2,1,0:T(8,128)(2,1)S(1)}, u32[]{:S(2)}, u32[]{:S(2)}) collective-permute-start(bf16[4,64,384]{2,1,0:T(8,128)(2,1)S(1)} %fusion.117), channel_id=1, source_target_pairs={{0,2},{1,3},{2,0},{3,1},{4,6},{5,7},{6,4},{7,5},{8,10},{9,11},{10,... | collective-permute-start | bytes 589832 | tf_op jit(solution)/shard_map/ppermute | solution.py:32
  107.6 5.6 %collective-permute-start.10 = (bf16[2,96,384]{2,1,0:T(8,128)(2,1)S(1)}, bf16[2,96,384]{2,1,0:T(8,128)(2,1)S(1)}, u32[]{:S(2)}, u32[]{:S(2)}) collective-permute-start(bf16[2,96,384]{2,1,0:T(8,128)(2,1)S(1)} %fusion.121), channel_id=1, source_target_pairs={{0,4},{1,5},{2,6},{3,7},{4,0},{5,1},{6,2},{7,3},{8,12},{9,13},{10,... | collective-permute-start | bytes 442376 | tf_op jit(solution)/shard_map/ppermute | solution.py:32
  110.2 5.7 %collective-permute-start.6 = (bf16[2,64,384]{2,1,0:T(8,128)(2,1)S(1)}, bf16[2,64,384]{2,1,0:T(8,128)(2,1)S(1)}, u32[]{:S(2)}, u32[]{:S(2)}) collective-permute-start(bf16[2,64,384]{2,1,0:T(8,128)(2,1)S(1)} %fusion.123), channel_id=1, source_target_pairs={{0,4},{1,5},{2,6},{3,7},{4,0},{5,1},{6,2},{7,3},{8,12},{9,13},{10,... | collective-permute-start | bytes 294920 | tf_op jit(solution)/shard_map/ppermute | solution.py:32
  113.3 5.7 %collective-permute-start.11 = (bf16[1,96,384]{2,1,0:T(8,128)(2,1)S(1)}, bf16[1,96,384]{2,1,0:T(8,128)(2,1)S(1)}, u32[]{:S(2)}, u32[]{:S(2)}) collective-permute-start(bf16[1,96,384]{2,1,0:T(8,128)(2,1)S(1)} %fusion.124), channel_id=1, source_target_pairs={{0,8},{1,9},{2,10},{3,11},{4,12},{5,13},{6,14},{7,15},{8,0},{9,1},... | collective-permute-start | bytes 221192 | tf_op jit(solution)/shard_map/ppermute | solution.py:32
  116.0 5.1 %collective-permute-start.7 = (bf16[1,64,384]{2,1,0:T(8,128)(2,1)S(1)}, bf16[1,64,384]{2,1,0:T(8,128)(2,1)S(1)}, u32[]{:S(2)}, u32[]{:S(2)}) collective-permute-start(bf16[1,64,384]{2,1,0:T(8,128)(2,1)S(1)} %fusion.125), channel_id=1, source_target_pairs={{0,8},{1,9},{2,10},{3,11},{4,12},{5,13},{6,14},{7,15},{8,0},{9,1},... | collective-permute-start | bytes 147464 | tf_op jit(solution)/shard_map/ppermute | solution.py:32
  (3 other events, 3.0 us)

commit v2 on v1

--- a/solution.py
+++ b/solution.py
@@ -69,10 +69,10 @@
     upper = lax.axis_index("seq") >= hops
 
     if paired:
-        w_far = jnp.where(upper, w_dilated[2], w_dilated[0])
-        w_all = jnp.concatenate([w_far, w_dilated[1]], axis=1)
+        w_far = lax.dynamic_index_in_dim(w_dilated, jnp.where(upper, 2, 0), 0, keepdims=False)
     else:
-        w_all = jnp.concatenate([w_dilated[0], w_dilated[2], w_dilated[1]], axis=1)
+        w_far = jnp.concatenate([w_dilated[0], w_dilated[2]], axis=1)
+    w_all = jnp.concatenate([w_far, w_dilated[1]], axis=1)
 
     def exchange(value):
         if paired:
@@ -90,9 +90,8 @@
         _, xhat, _ = normalize(b)
         act = gelu_fn(xhat * gain).astype(BF16)
         acts.append(act)
-        product = dot(act, w_all)
-        far = product[:, :-narrow].astype(BF16)
-        own.append(product[:, -narrow:])
+        far = dot(act, w_far).astype(BF16)
+        own.append(dot(act, w_dilated[1]))
         sent.append(exchange([far[:, :narrow], far[:, -narrow:]]))
 
     outs, hids, grads_pre, arrived = [], [], [], []
@@ -115,7 +114,28 @@
     early = jnp.concatenate(
         [centre_terms.reshape(n, shard, narrow), point_terms.reshape(n, shard, narrow)], axis=1
     )
-    early = reduced(early)[0] * scale
+    early = reduced(early, last=False)
+    arrived, early = lax.optimization_barrier((arrived, early))
+    if paired:
+        far_terms = dot_rows(act_all, jnp.concatenate([a[0] for a in arrived]))
+        late = reduced(far_terms.reshape(n, shard, narrow), last=False)
+    else:
+        zero_terms = dot_rows(act_all, jnp.concatenate([a[1] for a in arrived]))
+        two_terms = dot_rows(act_all, jnp.concatenate([a[0] for a in arrived]))
+        late = reduced(
+            jnp.concatenate(
+                [zero_terms.reshape(n, shard, narrow), two_terms.reshape(n, shard, narrow)], axis=1
+            ),
+            last=False,
+        )
+    keep, send = halves(jnp.concatenate([early, late], axis=1), n // 2)
+    keep, other = keep[0], swap(send, n // 2)[0].astype(F32)
+    early = (keep[: 2 * shard] + other[: 2 * shard]) * scale
+    keep, other = keep[2 * shard :], other[2 * shard :]
+    if paired:
+        first, final = jnp.where(upper, other, keep), jnp.where(upper, keep, other)
+    else:
+        first, final = keep[:shard] + other[:shard], keep[shard:] + other[shard:]
 
     grad_in, gain_terms = [], jnp.zeros((channels,), F32)
     for b in range(num_seqs):
@@ -137,26 +157,7 @@
         grad_in.append((cotangent[b].astype(F32) + part).astype(BF16))
     grad_inputs = jnp.stack(grad_in)
 
-    gain_block = jnp.pad(gain_terms.reshape(n, 1, shard), ((0, 0), (0, 15), (0, narrow - shard)))
-    if paired:
-        far_terms = dot_rows(act_all, jnp.concatenate([a[0] for a in arrived]))
-        late = jnp.concatenate([far_terms.reshape(n, shard, narrow), gain_block], axis=1)
-        late = reduced(late, last=False)
-        keep, send = halves(late, n // 2)
-        keep, other = keep[0], swap(send, n // 2)[0].astype(F32)
-        first = jnp.where(upper, other[:shard], keep[:shard])
-        final = jnp.where(upper, keep[:shard], other[:shard])
-        gain_sum = keep[shard, :shard] + other[shard, :shard]
-    else:
-        zero_terms = dot_rows(act_all, jnp.concatenate([a[1] for a in arrived]))
-        two_terms = dot_rows(act_all, jnp.concatenate([a[0] for a in arrived]))
-        late = jnp.concatenate(
-            [zero_terms.reshape(n, shard, narrow), two_terms.reshape(n, shard, narrow), gain_block],
-            axis=1,
-        )
-        late = reduced(late)[0]
-        first, final = late[:shard], late[shard : 2 * shard]
-        gain_sum = late[2 * shard, :shard]
+    gain_sum = reduced(gain_terms.reshape(n, 1, shard))[0, 0]
     grad_dilated = jnp.stack([first * scale, early[:shard], final * scale])
     return outputs, grad_inputs, grad_dilated, early[shard:].T, gain_sum * scale
 

time: 123 us -> 138 us (1.12)
  waiting for transfers between devices: 55.2 us -> 75.2 us
  other arithmetic: 17.5 us -> 14.9 us
    ppermute x12 -> x15, waiting for transfers between devices: 55.2 us -> 75.2 us  [swap(): return lax.ppermute(value, 'seq', [(s, s ^ bit) for s in range(n)])]
    dot_general x4 -> x6, matrix products: 3.59 us -> 9.48 us  [dot(): return jnp.dot(a, b, preferred_element_type=F32)]
    dot_general x4, matrix products: 14 us -> 9.97 us  [dot_last(): lax.dot_general(a, b, (((1,), (1,)), ((), ())), preferred_element_type=F32)]
    convert_element_type x2 -> x0, other arithmetic: 2.63 us -> none  [per_device(): hid = gelu_fn(pre).astype(BF16)]
    dot_general x3, matrix products: 7.84 us -> 5.33 us  [dot_rows(): lax.dot_general(a, b, (((0,), (0,)), ((), ())), preferred_element_type=F32)]
    convert_element_type x1 -> x2, other arithmetic: 1.63 us -> 4.08 us  [per_device(): act = gelu_fn(xhat * gain).astype(BF16)]
    squeeze x0 -> x1, local copies, waits for them, and re-layouts: none -> 2.18 us  [per_device(): own.append(dot(act, w_dilated[1]))]
    select_n x1 -> x0, other arithmetic: 1.55 us -> none  [per_device(): w_far = jnp.where(upper, w_dilated[2], w_dilated[0])]
  transfers between devices with their start and end apart: 12 -> 15, of which waited for: 7 -> 12; matrix products, arithmetic and copies ran while one was open for 31% -> 10% of each run, Pallas kernels for 0% -> 0%
where the time goes in v2:
time: 138 us
  waiting for transfers between devices  75.2 us (54%)
  matrix products  24.8 us (18%)
  other arithmetic  14.9 us (11%)
  starting transfers between devices  14.3 us (10%)
  local copies, waits for them, and re-layouts  7.29 us (5%)
    ppermute x15, waiting for transfers between devices, swap(): return lax.ppermute(value, 'seq', [(s, s ^ bit) for s in range(n)])  75.2 us
    ppermute x15, starting transfers between devices, swap(): return lax.ppermute(value, 'seq', [(s, s ^ bit) for s in range(n)])  14.3 us
    dot_general x4, matrix products, dot_last(): lax.dot_general(a, b, (((1,), (1,)), ((), ())), preferred_element_type=F32)  9.97 us
    dot_general x6, matrix products, dot(): return jnp.dot(a, b, preferred_element_type=F32)  9.48 us
    dot_general x3, matrix products, dot_rows(): lax.dot_general(a, b, (((0,), (0,)), ((), ())), preferred_element_type=F32)  5.33 us
    convert_element_type x2, other arithmetic, per_device(): act = gelu_fn(xhat * gain).astype(BF16)  4.08 us
  transfers between devices with their start and end apart: 15, of which 12 were waited for; matrix products, arithmetic and copies ran while one was open for 10% of the time, Pallas kernels for 0%

profile of v2, /device:TPU:0, one launch (start us, length us, event | category | flops | bytes accessed | tf_op | source)
XLA Modules:
  0.0 137.6 jit_solution(6155336973029384912)
XLA Ops:
  0.7 1.8 %convert_reduce_fusion.1 = (f32[512]{0:T(512)S(1)}, f32[512]{0:T(512)S(1)}) fusion(bf16[2,512,768]{2,1,0:T(8,128)(2,1)} %param.5), kind=kLoop, calls=%fused_computation.6 | loop fusion | flops 1571840 | bytes 1576960 | tf_op jit(solution)/shard_map/reduce_sum | solution.py:84
  3.2 2.2 %slice_bitcast_fusion.4 = (bf16[768,384]{1,0:T(8,128)(2,1)}, bf16[768,384]{1,0:T(8,128)(2,1)S(1)}) fusion(bf16[3,768,384]{2,1,0:T(8,128)(2,1)} %param.7, s32[]{:T(128)S(6)} %select_n.276), kind=kLoop, calls=%fused_computation.166 | loop fusion | bytes 2359300 | tf_op jit(solution)/shard_map/squeeze | solution.py:94
  5.4 1.6 %fusion.96 = (bf16[512,768]{1,0:T(8,128)(2,1)S(1)}, bf16[512,768]{1,0:T(8,128)(2,1)S(1)}) fusion(f32[768]{0:T(1024)S(1)} %copy-done.20, f32[512]{0:T(512)S(1)} %add_rsqrt_fusion.1, f32[512]{0:T(512)S(1)} %get-tuple-element.41, bf16[2,512,768]{2,1,0:T(8,128)(2,1)S(1)} %copy-done.1, f32[512]{0:T(512)S(1)} %add_rsqrt_fusion, f32[512]{0:T(512)S(1)} %get-tuple-element.40), kind=kLoop, calls=%fused_computation.126 | loop fusion | flops 10223616 | bytes 3156992 | tf_op jit(solution)/shard_map/convert_element_type | solution.py:91
  8.3 4.0 %collective-permute-start = (bf16[512,384]{1,0:T(8,128)(2,1)}, bf16[512,384]{1,0:T(8,128)(2,1)S(1)}, u32[]{:S(2)}, u32[]{:S(2)}) collective-permute-start(bf16[512,384]{1,0:T(8,128)(2,1)} %convolution_convert_fusion.1), channel_id=1, source_target_pairs={{0,8},{1,9},{2,10},{3,11},{4,12},{5,13},{6,14},{7,15},{8,0},{9,1},... | collective-permute-start | bytes 1179656 | tf_op jit(solution)/shard_map/ppermute | solution.py:32
  13.7 2.5 %fusion.24 = (bf16[512,768]{1,0:T(8,128)(2,1)}, bf16[512,768]{1,0:T(8,128)(2,1)}) fusion(f32[768]{0:T(1024)S(1)} %copy-done.20, f32[512]{0:T(512)S(1)} %add_rsqrt_fusion.1, f32[512]{0:T(512)S(1)} %get-tuple-element.41, bf16[2,512,768]{2,1,0:T(8,128)(2,1)S(1)} %copy-done.1, f32[512]{0:T(512)S(1)} %add_rsqrt_fusion, f32[512]{0:T(512)S(1)} %get-tuple-element.40), kind=kLoop, calls=%fused_computation.38 | loop fusion | flops 10223616 | bytes 3156992 | tf_op jit(solution)/shard_map/convert_element_type | solution.py:91
  16.2 23.2 %collective-permute-done = bf16[512,384]{1,0:T(8,128)(2,1)S(1)} collective-permute-done((bf16[512,384]{1,0:T(8,128)(2,1)}, bf16[512,384]{1,0:T(8,128)(2,1)S(1)}, u32[]{:S(2)}, u32[]{:S(2)}) %collective-permute-start) | collective-permute-done | bytes 393248 | tf_op jit(solution)/shard_map/ppermute | solution.py:32
  39.4 3.0 %multiply_convert_fusion.1 = (bf16[512,384]{1,0:T(8,128)(2,1)S(1)}, f32[512,384]{1,0:T(8,128)}) fusion(bf16[512,384]{1,0:T(8,128)(2,1)S(1)} %collective-permute-done, bf16[512,768]{1,0:T(8,128)(2,1)} %copy-done.12, bf16[3,768,384]{2,1,0:T(8,128)(2,1)} %param.7), kind=kOutput, calls=%fused_computation.152 | convolution fusion | flops 304152576 | bytes 2949120 | tf_op jit(solution)/shard_map/dot_general | solution.py:19
  42.4 4.7 %collective-permute-done.1 = bf16[512,384]{1,0:T(8,128)(2,1)} collective-permute-done((bf16[512,384]{1,0:T(8,128)(2,1)}, bf16[512,384]{1,0:T(8,128)(2,1)}, u32[]{:S(2)}, u32[]{:S(2)}) %collective-permute-start.1) | collective-permute-done | bytes 393248 | tf_op jit(solution)/shard_map/ppermute | solution.py:32
  47.1 2.7 %multiply_convert_fusion = (bf16[512,384]{1,0:T(8,128)(2,1)S(1)}, f32[512,384]{1,0:T(8,128)}) fusion(bf16[512,384]{1,0:T(8,128)(2,1)} %collective-permute-done.1, bf16[512,768]{1,0:T(8,128)(2,1)S(1)} %get-tuple-element.30, bf16[3,768,384]{2,1,0:T(8,128)(2,1)} %param.7), kind=kOutput, calls=%fused_computation.150 | convolution fusion | flops 304152576 | bytes 2949120 | tf_op jit(solution)/shard_map/dot_general | solution.py:19
  50.5 1.8 %convolution_bitcast_fusion = f32[768,384]{0,1:T(8,128)} fusion(bf16[1024,768]{1,0:T(8,128)(2,1)S(1)} %bitcast.373, bf16[512,384]{1,0:T(8,128)(2,1)S(1)} %get-tuple-element.35, bf16[512,384]{1,0:T(8,128)(2,1)S(1)} %get-tuple-element.37), kind=kOutput, calls=%fused_computation.91 | convolution fusion | flops 605552640 | bytes 3538944 | tf_op jit(solution)/shard_map/dot_general | solution.py:23
  52.4 1.6 %copy.50 = f32[768,384]{1,0:T(8,128)S(1)} copy(f32[768,384]{0,1:T(8,128)} %convolution_bitcast_fusion) | data formatting | bytes 2359296 | tf_op jit(solution)/shard_map/dot_general | solution.py:23
  54.0 2.6 %fusion.87 = bf16[512,384]{1,0:T(8,128)(2,1)S(1)} fusion(bf16[384,768]{1,0:T(8,128)(2,1)S(1)} %copy-done, bf16[2,512,768]{2,1,0:T(8,128)(2,1)} %param.9, f32[512,384]{1,0:T(8,128)} %get-tuple-element.38, bf16[512,384]{1,0:T(8,128)(2,1)} %copy-done.27), kind=kOutput, calls=%fused_computation.117 | convolution fusion | flops 306315264 | bytes 2949120 | tf_op jit(solution)/shard_map/dot_general | solution.py:27
  56.7 2.1 %fusion.94 = bf16[512,384]{1,0:T(8,128)(2,1)S(1)} fusion(bf16[384,768]{1,0:T(8,128)(2,1)S(1)} %copy-done, bf16[2,512,768]{2,1,0:T(8,128)(2,1)S(1)} %copy-done.4, f32[512,384]{1,0:T(8,128)S(1)} %copy-done.28, bf16[512,384]{1,0:T(8,128)(2,1)} %collective-permute-done.1), kind=kOutput, calls=%fused_computation.124 | convolution fusion | flops 306315264 | bytes 2949120 | tf_op jit(solution)/shard_map/dot_general | solution.py:27
  61.8 2.9 %collective-permute-start.3 = (bf16[512,384]{1,0:T(8,128)(2,1)}, bf16[512,384]{1,0:T(8,128)(2,1)S(1)}, u32[]{:S(2)}, u32[]{:S(2)}) collective-permute-start(bf16[512,384]{1,0:T(8,128)(2,1)} %copy-done.23), channel_id=1, source_target_pairs={{0,8},{1,9},{2,10},{3,11},{4,12},{5,13},{6,14},{7,15},{8,0},{9,1},... | collective-permute-start | bytes 1179656 | tf_op jit(solution)/shard_map/ppermute | solution.py:32
  64.7 1.6 %fusion.78 = f32[8,96,384]{2,1,0:T(8,128)S(1)} fusion(bf16[8,96,384]{2,1,0:T(8,128)(2,1)} %collective-permute-done.4, pred[]{:T(512)S(6)} %ne.10, f32[8,2,48,384]{3,2,1,0:T(8,128)S(1)} %bitcast.360, f32[8,2,48,384]{3,2,1,0:T(8,128)} %bitcast.364), kind=kLoop, calls=%fused_computation.103 | loop fusion | flops 1474560 | bytes 4128769 | tf_op jit(solution)/shard_map/add | solution.py:55
  66.4 1.6 %collective-permute-start.5 = (bf16[4,96,384]{2,1,0:T(8,128)(2,1)S(1)}, bf16[4,96,384]{2,1,0:T(8,128)(2,1)S(1)}, u32[]{:S(2)}, u32[]{:S(2)}) collective-permute-start(bf16[4,96,384]{2,1,0:T(8,128)(2,1)S(1)} %fusion.131), channel_id=1, source_target_pairs={{0,2},{1,3},{2,0},{3,1},{4,6},{5,7},{6,4},{7,5},{8,10},{9,11},{10,... | collective-permute-start | bytes 884744 | tf_op jit(solution)/shard_map/ppermute | solution.py:32
  69.2 6.1 %collective-permute-done.5 = bf16[4,96,384]{2,1,0:T(8,128)(2,1)S(1)} collective-permute-done((bf16[4,96,384]{2,1,0:T(8,128)(2,1)S(1)}, bf16[4,96,384]{2,1,0:T(8,128)(2,1)S(1)}, u32[]{:S(2)}, u32[]{:S(2)}) %collective-permute-start.5) | collective-permute-done | bytes 294944 | tf_op jit(solution)/shard_map/ppermute | solution.py:32
  75.4 1.6 %collective-permute-start.6 = (bf16[2,96,384]{2,1,0:T(8,128)(2,1)S(1)}, bf16[2,96,384]{2,1,0:T(8,128)(2,1)S(1)}, u32[]{:S(2)}, u32[]{:S(2)}) collective-permute-start(bf16[2,96,384]{2,1,0:T(8,128)(2,1)S(1)} %fusion.137), channel_id=1, source_target_pairs={{0,4},{1,5},{2,6},{3,7},{4,0},{5,1},{6,2},{7,3},{8,12},{9,13},{10,... | collective-permute-start | bytes 442376 | tf_op jit(solution)/shard_map/ppermute | solution.py:32
  78.3 4.7 %collective-permute-done.6 = bf16[2,96,384]{2,1,0:T(8,128)(2,1)S(1)} collective-permute-done((bf16[2,96,384]{2,1,0:T(8,128)(2,1)S(1)}, bf16[2,96,384]{2,1,0:T(8,128)(2,1)S(1)}, u32[]{:S(2)}, u32[]{:S(2)}) %collective-permute-start.6) | collective-permute-done | bytes 147488 | tf_op jit(solution)/shard_map/ppermute | solution.py:32
  83.0 8.7 %collective-permute-done.2 = bf16[512,384]{1,0:T(8,128)(2,1)S(1)} collective-permute-done((bf16[512,384]{1,0:T(8,128)(2,1)}, bf16[512,384]{1,0:T(8,128)(2,1)S(1)}, u32[]{:S(2)}, u32[]{:S(2)}) %collective-permute-start.2) | collective-permute-done | bytes 393248 | tf_op jit(solution)/shard_map/ppermute | solution.py:32
  91.7 8.0 %collective-permute-done.3 = bf16[512,384]{1,0:T(8,128)(2,1)S(1)} collective-permute-done((bf16[512,384]{1,0:T(8,128)(2,1)}, bf16[512,384]{1,0:T(8,128)(2,1)S(1)}, u32[]{:S(2)}, u32[]{:S(2)}) %collective-permute-start.3) | collective-permute-done | bytes 393248 | tf_op jit(solution)/shard_map/ppermute | solution.py:32
  100.5 1.7 %fusion.53 = f32[512,768]{1,0:T(8,128)S(1)} fusion(bf16[512,384]{1,0:T(8,128)(2,1)S(1)} %copy-done.24, bf16[512,384]{1,0:T(8,128)(2,1)S(1)} %collective-permute-done.3, f32[512]{0:T(512)S(1)} %add_rsqrt_fusion, f32[768]{0:T(1024)S(1)} %copy-done.20, f32[512]{0:T(512)S(1)} %get-tuple-element.40, bf16[768,384]{1,0:T(8,128)(2,1)S(1)} %copy-done.13, ...), kind=kOutput, calls=%fused_computation.67 | convolution fusion | flops 616955904 | bytes 4332544 | tf_op jit(solution)/shard_map/dot_general | solution.py:27
  102.2 3.6 %fusion.32 = (f32[768]{0:T(1024)S(1)}, f32[512]{0:T(512)S(1)}, f32[512]{0:T(512)S(1)}, f32[768]{0:T(1024)S(1)}, f32[512]{0:T(512)S(1)}, /*index=5*/f32[512]{0:T(512)S(1)}, f32[512,768]{1,0:T(8,128)}) fusion(f32[512]{0:T(512)S(1)} %add_rsqrt_fusion.1, f32[512]{0:T(512)S(1)} %get-tuple-element.41, bf16[2,512,768]{2,1,0:T(8,128)(2,1)S(1)} %copy-done.1, ...), kind=kOutput, calls=%fused_computation.46 | convolution fusion | flops 622850560 | bytes 6710272 | tf_op jit(solution)/shard_map/dot_general | solution.py:27
  106.0 2.5 %fusion.79 = f32[768,384]{1,0:T(8,128)S(1)} fusion(bf16[512,768]{1,0:T(8,128)(2,1)} %get-tuple-element.28, bf16[512,768]{1,0:T(8,128)(2,1)S(1)} %copy-done.10, bf16[512,384]{1,0:T(8,128)(2,1)} %copy-done.26, bf16[512,384]{1,0:T(8,128)(2,1)} %copy-done.25), kind=kOutput, calls=%fused_computation.109 | convolution fusion | flops 608698368 | bytes 3538944 | tf_op jit(solution)/shard_map/dot_general | solution.py:23
  109.2 1.4 %fusion.98 = (bf16[1,512,768]{2,1,0:T(8,128)(2,1)S(1)}, bf16[1,512,768]{2,1,0:T(8,128)(2,1)S(1)}) fusion(f32[512,768]{1,0:T(8,128)S(1)} %copy-done.8, f32[512]{0:T(512)S(1)} %broadcast_multiply_fusion.2, f32[512]{0:T(512)S(1)} %broadcast_multiply_fusion.3, f32[768]{0:T(1024)S(1)} %copy-done.20, f32[512]{0:T(512)S(1)} %add_rsqrt_fusion.1, ...), kind=kLoop, calls=%fused_computation.128 | loop fusion | flops 8650752 | bytes 7883776 | tf_op jit(solution)/shard_map/stack | solution.py:158
  112.0 1.6 %collective-permute-start.12 = (bf16[4,1,48]{2,0,1:T(4,128)(2,1)S(1)}, bf16[4,1,48]{2,0,1:T(4,128)(2,1)S(1)}, u32[]{:S(2)}, u32[]{:S(2)}) collective-permute-start(bf16[4,1,48]{2,0,1:T(4,128)(2,1)S(1)} %bitcast.382), channel_id=1, source_target_pairs={{0,2},{1,3},{2,0},{3,1},{4,6},{5,7},{6,4},{7,5},{8,10},{9,11},{10,... | collective-permute-start | bytes 1160 | tf_op jit(solution)/shard_map/ppermute | solution.py:32
  113.6 2.0 %collective-permute-done.12 = bf16[4,1,48]{2,0,1:T(4,128)(2,1)S(1)} collective-permute-done((bf16[4,1,48]{2,0,1:T(4,128)(2,1)S(1)}, bf16[4,1,48]{2,0,1:T(4,128)(2,1)S(1)}, u32[]{:S(2)}, u32[]{:S(2)}) %collective-permute-start.12) | collective-permute-done | bytes 416 | tf_op jit(solution)/shard_map/ppermute | solution.py:32
  115.7 3.5 %collective-permute-done.13 = bf16[2,1,48]{2,0,1:T(2,128)(2,1)S(1)} collective-permute-done((bf16[2,1,48]{2,0,1:T(2,128)(2,1)S(1)}, bf16[2,1,48]{2,0,1:T(2,128)(2,1)S(1)}, u32[]{:S(2)}, u32[]{:S(2)}) %collective-permute-start.13) | collective-permute-done | bytes 224 | tf_op jit(solution)/shard_map/ppermute | solution.py:32
  119.4 1.6 %collective-permute-start.8 = (bf16[4,48,384]{2,1,0:T(8,128)(2,1)S(1)}, bf16[4,48,384]{2,1,0:T(8,128)(2,1)S(1)}, u32[]{:S(2)}, u32[]{:S(2)}) collective-permute-start(bf16[4,48,384]{2,1,0:T(8,128)(2,1)S(1)} %fusion.138), channel_id=1, source_target_pairs={{0,2},{1,3},{2,0},{3,1},{4,6},{5,7},{6,4},{7,5},{8,10},{9,11},{10,... | collective-permute-start | bytes 442376 | tf_op jit(solution)/shard_map/ppermute | solution.py:32
  121.0 3.6 %collective-permute-done.8 = bf16[4,48,384]{2,1,0:T(8,128)(2,1)S(1)} collective-permute-done((bf16[4,48,384]{2,1,0:T(8,128)(2,1)S(1)}, bf16[4,48,384]{2,1,0:T(8,128)(2,1)S(1)}, u32[]{:S(2)}, u32[]{:S(2)}) %collective-permute-start.8) | collective-permute-done | bytes 147488 | tf_op jit(solution)/shard_map/ppermute | solution.py:32
  126.0 3.4 %collective-permute-done.9 = bf16[2,48,384]{2,1,0:T(8,128)(2,1)S(1)} collective-permute-done((bf16[2,48,384]{2,1,0:T(8,128)(2,1)S(1)}, bf16[2,48,384]{2,1,0:T(8,128)(2,1)S(1)}, u32[]{:S(2)}, u32[]{:S(2)}) %collective-permute-start.9) | collective-permute-done | bytes 73760 | tf_op jit(solution)/shard_map/ppermute | solution.py:32
  129.6 6.6 %collective-permute-done.10 = bf16[1,144,384]{2,1,0:T(8,128)(2,1)S(1)} collective-permute-done((bf16[1,144,384]{2,1,0:T(8,128)(2,1)S(1)}, bf16[1,144,384]{2,1,0:T(8,128)(2,1)S(1)}, u32[]{:S(2)}, u32[]{:S(2)}) %collective-permute-start.10) | collective-permute-done | bytes 110624 | tf_op jit(solution)/shard_map/ppermute | solution.py:32
  (121 shorter events, 15.9 us)
Async XLA Ops:
  0.6 53.4 %copy-start = (bf16[384,768]{1,0:T(8,128)(2,1)S(1)}, bf16[384,768]{1,0:T(8,128)(2,1)}, u32[]{:S(2)}) copy-start(bf16[384,768]{1,0:T(8,128)(2,1)} %param.8) | copy-start | bytes 1769476
  5.4 7.0 %copy-start.14 = (bf16[768,384]{1,0:T(8,128)(2,1)}, bf16[768,384]{1,0:T(8,128)(2,1)S(1)}, u32[]{:S(2)}) copy-start(bf16[768,384]{1,0:T(8,128)(2,1)S(1)} %get-tuple-element.26) | copy-start | bytes 1769476
  7.0 6.7 %copy-start.12 = (bf16[512,768]{1,0:T(8,128)(2,1)}, bf16[512,768]{1,0:T(8,128)(2,1)S(1)}, u32[]{:S(2)}) copy-start(bf16[512,768]{1,0:T(8,128)(2,1)S(1)} %get-tuple-element.29) | copy-start | bytes 2359300
  8.3 31.0 %collective-permute-start = (bf16[512,384]{1,0:T(8,128)(2,1)}, bf16[512,384]{1,0:T(8,128)(2,1)S(1)}, u32[]{:S(2)}, u32[]{:S(2)}) collective-permute-start(bf16[512,384]{1,0:T(8,128)(2,1)} %convolution_convert_fusion.1), channel_id=1, source_target_pairs={{0,8},{1,9},{2,10},{3,11},{4,12},{5,13},{6,14},{7,15},{8,0},{9,1},... | collective-permute-start | bytes 1179656 | tf_op jit(solution)/shard_map/ppermute | solution.py:32
  13.7 33.4 %collective-permute-start.1 = (bf16[512,384]{1,0:T(8,128)(2,1)}, bf16[512,384]{1,0:T(8,128)(2,1)}, u32[]{:S(2)}, u32[]{:S(2)}) collective-permute-start(bf16[512,384]{1,0:T(8,128)(2,1)} %convolution_convert_fusion), channel_id=1, source_target_pairs={{0,8},{1,9},{2,10},{3,11},{4,12},{5,13},{6,14},{7,15},{8,0},{9,1},... | collective-permute-start | bytes 1179656 | tf_op jit(solution)/shard_map/ppermute | solution.py:32
  39.4 3.0 %copy-start.27 = (bf16[512,384]{1,0:T(8,128)(2,1)}, bf16[512,384]{1,0:T(8,128)(2,1)S(1)}, u32[]{:S(2)}) copy-start(bf16[512,384]{1,0:T(8,128)(2,1)S(1)} %collective-permute-done) | copy-start | bytes 1179652
  42.4 7.4 %copy-start.16 = (bf16[512,384]{1,0:T(8,128)(2,1)}, bf16[512,384]{1,0:T(8,128)(2,1)S(1)}, u32[]{:S(2)}) copy-start(bf16[512,384]{1,0:T(8,128)(2,1)S(1)} %get-tuple-element.37) | copy-start | bytes 1179652
  42.4 8.2 %copy-start.3 = (bf16[2,512,768]{2,1,0:T(8,128)(2,1)S(1)}, bf16[2,512,768]{2,1,0:T(8,128)(2,1)}, u32[]{:S(2)}) copy-start(bf16[2,512,768]{2,1,0:T(8,128)(2,1)} %param.9) | copy-start | bytes 4718596
  54.0 2.6 %copy-start.4 = (bf16[2,512,768]{2,1,0:T(8,128)(2,1)S(1)}, bf16[2,512,768]{2,1,0:T(8,128)(2,1)}, u32[]{:S(2)}) copy-start(bf16[2,512,768]{2,1,0:T(8,128)(2,1)} %param.9) | copy-start | bytes 4718596
  61.8 2.9 %collective-permute-start.4 = (bf16[8,96,384]{2,1,0:T(8,128)(2,1)}, bf16[8,96,384]{2,1,0:T(8,128)(2,1)}, u32[]{:S(2)}, u32[]{:S(2)}) collective-permute-start(bf16[8,96,384]{2,1,0:T(8,128)(2,1)} %fusion.130), channel_id=1, source_target_pairs={{0,1},{1,0},{2,3},{3,2},{4,5},{5,4},{6,7},{7,6},{8,9},{9,8},{10,11... | collective-permute-start | bytes 1769480 | tf_op jit(solution)/shard_map/ppermute | solution.py:32
  61.8 6.2 %copy-start.17 = (bf16[512,384]{1,0:T(8,128)(2,1)S(1)}, bf16[512,384]{1,0:T(8,128)(2,1)}, u32[]{:S(2)}) copy-start(bf16[512,384]{1,0:T(8,128)(2,1)} %copy-done.16) | copy-start | bytes 1179652
  61.8 29.9 %collective-permute-start.2 = (bf16[512,384]{1,0:T(8,128)(2,1)}, bf16[512,384]{1,0:T(8,128)(2,1)S(1)}, u32[]{:S(2)}, u32[]{:S(2)}) collective-permute-start(bf16[512,384]{1,0:T(8,128)(2,1)} %copy-done.21), channel_id=1, source_target_pairs={{0,8},{1,9},{2,10},{3,11},{4,12},{5,13},{6,14},{7,15},{8,0},{9,1},... | collective-permute-start | bytes 1179656 | tf_op jit(solution)/shard_map/ppermute | solution.py:32
  61.8 37.9 %collective-permute-start.3 = (bf16[512,384]{1,0:T(8,128)(2,1)}, bf16[512,384]{1,0:T(8,128)(2,1)S(1)}, u32[]{:S(2)}, u32[]{:S(2)}) collective-permute-start(bf16[512,384]{1,0:T(8,128)(2,1)} %copy-done.23), channel_id=1, source_target_pairs={{0,8},{1,9},{2,10},{3,11},{4,12},{5,13},{6,14},{7,15},{8,0},{9,1},... | collective-permute-start | bytes 1179656 | tf_op jit(solution)/shard_map/ppermute | solution.py:32
  66.4 8.9 %collective-permute-start.5 = (bf16[4,96,384]{2,1,0:T(8,128)(2,1)S(1)}, bf16[4,96,384]{2,1,0:T(8,128)(2,1)S(1)}, u32[]{:S(2)}, u32[]{:S(2)}) collective-permute-start(bf16[4,96,384]{2,1,0:T(8,128)(2,1)S(1)} %fusion.131), channel_id=1, source_target_pairs={{0,2},{1,3},{2,0},{3,1},{4,6},{5,7},{6,4},{7,5},{8,10},{9,11},{10,... | collective-permute-start | bytes 884744 | tf_op jit(solution)/shard_map/ppermute | solution.py:32
  75.4 25.0 %copy-start.13 = (bf16[768,384]{1,0:T(8,128)(2,1)S(1)}, bf16[768,384]{1,0:T(8,128)(2,1)}, u32[]{:S(2)}) copy-start(bf16[768,384]{1,0:T(8,128)(2,1)} %get-tuple-element.25) | copy-start | bytes 1769476
  75.4 25.0 %copy-start.15 = (bf16[768,384]{1,0:T(8,128)(2,1)S(1)}, bf16[768,384]{1,0:T(8,128)(2,1)}, u32[]{:S(2)}) copy-start(bf16[768,384]{1,0:T(8,128)(2,1)} %copy-done.14) | copy-start | bytes 1769476
  75.4 25.0 %copy-start.24 = (bf16[512,384]{1,0:T(8,128)(2,1)S(1)}, bf16[512,384]{1,0:T(8,128)(2,1)}, u32[]{:S(2)}) copy-start(bf16[512,384]{1,0:T(8,128)(2,1)} %copy-done.23) | copy-start | bytes 1179652
  75.4 7.5 %collective-permute-start.6 = (bf16[2,96,384]{2,1,0:T(8,128)(2,1)S(1)}, bf16[2,96,384]{2,1,0:T(8,128)(2,1)S(1)}, u32[]{:S(2)}, u32[]{:S(2)}) collective-permute-start(bf16[2,96,384]{2,1,0:T(8,128)(2,1)S(1)} %fusion.137), channel_id=1, source_target_pairs={{0,4},{1,5},{2,6},{3,7},{4,0},{5,1},{6,2},{7,3},{8,12},{9,13},{10,... | collective-permute-start | bytes 442376 | tf_op jit(solution)/shard_map/ppermute | solution.py:32
  91.7 10.5 %copy-start.25 = (bf16[512,384]{1,0:T(8,128)(2,1)}, bf16[512,384]{1,0:T(8,128)(2,1)S(1)}, u32[]{:S(2)}) copy-start(bf16[512,384]{1,0:T(8,128)(2,1)S(1)} %collective-permute-done.2) | copy-start | bytes 1179652
  102.2 3.7 %copy-start.6 = (f32[512,768]{1,0:T(8,128)}, f32[512,768]{1,0:T(8,128)S(1)}, u32[]{:S(2)}) copy-start(f32[512,768]{1,0:T(8,128)S(1)} %fusion.53) | copy-start | bytes 4718596
  102.2 3.8 %copy-start.10 = (bf16[512,768]{1,0:T(8,128)(2,1)S(1)}, bf16[512,768]{1,0:T(8,128)(2,1)}, u32[]{:S(2)}) copy-start(bf16[512,768]{1,0:T(8,128)(2,1)} %get-tuple-element.27) | copy-start | bytes 2359300
  106.0 3.3 %copy-start.5 = (bf16[2,512,768]{2,1,0:T(8,128)(2,1)S(1)}, bf16[2,512,768]{2,1,0:T(8,128)(2,1)}, u32[]{:S(2)}) copy-start(bf16[2,512,768]{2,1,0:T(8,128)(2,1)} %param.9) | copy-start | bytes 4718596
  106.0 3.3 %copy-start.7 = (f32[512,768]{1,0:T(8,128)S(1)}, f32[512,768]{1,0:T(8,128)}, u32[]{:S(2)}) copy-start(f32[512,768]{1,0:T(8,128)} %copy-done.6) | copy-start | bytes 4718596
  106.0 3.3 %copy-start.8 = (f32[512,768]{1,0:T(8,128)S(1)}, f32[512,768]{1,0:T(8,128)}, u32[]{:S(2)}) copy-start(f32[512,768]{1,0:T(8,128)} %get-tuple-element.39) | copy-start | bytes 4718596
  108.5 3.5 %collective-permute-start.11 = (bf16[8,1,48]{2,0,1:T(8,128)(2,1)S(1)}, bf16[8,1,48]{2,0,1:T(8,128)(2,1)S(1)}, u32[]{:S(2)}, u32[]{:S(2)}) collective-permute-start(bf16[8,1,48]{2,0,1:T(8,128)(2,1)S(1)} %bitcast.381), channel_id=1, source_target_pairs={{0,1},{1,0},{2,3},{3,2},{4,5},{5,4},{6,7},{7,6},{8,9},{9,8},{10,11... | collective-permute-start | bytes 2312 | tf_op jit(solution)/shard_map/ppermute | solution.py:32
  108.6 10.6 %collective-permute-start.7 = (bf16[8,48,384]{2,1,0:T(8,128)(2,1)S(1)}, bf16[8,48,384]{2,1,0:T(8,128)(2,1)S(1)}, u32[]{:S(2)}, u32[]{:S(2)}) collective-permute-start(bf16[8,48,384]{2,1,0:T(8,128)(2,1)S(1)} %fusion.132), channel_id=1, source_target_pairs={{0,1},{1,0},{2,3},{3,2},{4,5},{5,4},{6,7},{7,6},{8,9},{9,8},{10,11... | collective-permute-start | bytes 884744 | tf_op jit(solution)/shard_map/ppermute | solution.py:32
  112.0 3.6 %collective-permute-start.12 = (bf16[4,1,48]{2,0,1:T(4,128)(2,1)S(1)}, bf16[4,1,48]{2,0,1:T(4,128)(2,1)S(1)}, u32[]{:S(2)}, u32[]{:S(2)}) collective-permute-start(bf16[4,1,48]{2,0,1:T(4,128)(2,1)S(1)} %bitcast.382), channel_id=1, source_target_pairs={{0,2},{1,3},{2,0},{3,1},{4,6},{5,7},{6,4},{7,5},{8,10},{9,11},{10,... | collective-permute-start | bytes 1160 | tf_op jit(solution)/shard_map/ppermute | solution.py:32
  115.6 3.6 %collective-permute-start.13 = (bf16[2,1,48]{2,0,1:T(2,128)(2,1)S(1)}, bf16[2,1,48]{2,0,1:T(2,128)(2,1)S(1)}, u32[]{:S(2)}, u32[]{:S(2)}) collective-permute-start(bf16[2,1,48]{2,0,1:T(2,128)(2,1)S(1)} %bitcast.383), channel_id=1, source_target_pairs={{0,4},{1,5},{2,6},{3,7},{4,0},{5,1},{6,2},{7,3},{8,12},{9,13},{10,... | collective-permute-start | bytes 584 | tf_op jit(solution)/shard_map/ppermute | solution.py:32
  119.4 5.2 %collective-permute-start.8 = (bf16[4,48,384]{2,1,0:T(8,128)(2,1)S(1)}, bf16[4,48,384]{2,1,0:T(8,128)(2,1)S(1)}, u32[]{:S(2)}, u32[]{:S(2)}) collective-permute-start(bf16[4,48,384]{2,1,0:T(8,128)(2,1)S(1)} %fusion.138), channel_id=1, source_target_pairs={{0,2},{1,3},{2,0},{3,1},{4,6},{5,7},{6,4},{7,5},{8,10},{9,11},{10,... | collective-permute-start | bytes 442376 | tf_op jit(solution)/shard_map/ppermute | solution.py:32
  121.0 4.4 %collective-permute-start.14 = (bf16[1,1,48]{2,1,0:T(2,128)(2,1)S(1)}, bf16[1,1,48]{2,1,0:T(2,128)(2,1)S(1)}, u32[]{:S(2)}, u32[]{:S(2)}) collective-permute-start(bf16[1,1,48]{2,1,0:T(2,128)(2,1)S(1)} %fusion.149), channel_id=1, source_target_pairs={{0,8},{1,9},{2,10},{3,11},{4,12},{5,13},{6,14},{7,15},{8,0},{9,1},... | collective-permute-start | bytes 296 | tf_op jit(solution)/shard_map/ppermute | solution.py:32
  124.7 4.7 %collective-permute-start.9 = (bf16[2,48,384]{2,1,0:T(8,128)(2,1)S(1)}, bf16[2,48,384]{2,1,0:T(8,128)(2,1)S(1)}, u32[]{:S(2)}, u32[]{:S(2)}) collective-permute-start(bf16[2,48,384]{2,1,0:T(8,128)(2,1)S(1)} %fusion.141), channel_id=1, source_target_pairs={{0,4},{1,5},{2,6},{3,7},{4,0},{5,1},{6,2},{7,3},{8,12},{9,13},{10,... | collective-permute-start | bytes 221192 | tf_op jit(solution)/shard_map/ppermute | solution.py:32
  129.5 6.7 %collective-permute-start.10 = (bf16[1,144,384]{2,1,0:T(8,128)(2,1)S(1)}, bf16[1,144,384]{2,1,0:T(8,128)(2,1)S(1)}, u32[]{:S(2)}, u32[]{:S(2)}) collective-permute-start(bf16[1,144,384]{2,1,0:T(8,128)(2,1)S(1)} %fusion.140), channel_id=1, source_target_pairs={{0,8},{1,9},{2,10},{3,11},{4,12},{5,13},{6,14},{7,15},{8,0},{9,1},... | collective-permute-start | bytes 331784 | tf_op jit(solution)/shard_map/ppermute | solution.py:32
  (12 other events, 20.8 us)

commit v3 on v1

--- a/solution.py
+++ b/solution.py
@@ -1,6 +1,8 @@
 import jax
 import jax.numpy as jnp
 from jax import lax
+from jax.experimental import pallas as pl
+from jax.experimental.pallas import tpu as pltpu
 from jax.sharding import PartitionSpec as P
 
 DILATION = 4096
@@ -160,6 +162,263 @@
     grad_dilated = jnp.stack([first * scale, early[:shard], final * scale])
     return outputs, grad_inputs, grad_dilated, early[shard:].T, gain_sum * scale
 
+CHUNKS = 4
+ROOT = 0.7978845608028654
+
+
+def gelu_parts(v):
+    square = v * v
+    t = jnp.tanh(ROOT * v * (1.0 + 0.044715 * square))
+    half = 0.5 * (1.0 + t)
+    slope = half + 0.5 * v * (1.0 - t * t) * (ROOT * (1.0 + 3 * 0.044715 * square))
+    return v * half, slope
+
+
+def block_kernel(
+    n, x_ref, gain_ref, w_ref, wp_ref, cot_ref,
+    out_ref, gin_ref, gd_ref, gp_ref, gg_ref,
+    act, own, p_send, p_recv, q, q_recv, hid, slope, mean_s, inv_s,
+    early, late, gain_acc, e_send, e_recv, l_send, l_recv, g_send, g_recv,
+    p_sems, q_sems, e_sems, l_sems, g_sems,
+):
+    me = lax.axis_index("seq")
+    rows, channels = x_ref.shape
+    narrow = wp_ref.shape[0]
+    shard = channels // n
+    size = rows // CHUNKS
+    bits, bit = [], 1
+    while bit < n:
+        bits.append(bit)
+        bit *= 2
+    mine = [(me // b) % 2 for b in bits]
+    partners = [me + b * (1 - 2 * m) for b, m in zip(bits, mine)]
+    upper = mine[-1]
+    far_tap = 2 * upper
+    scale = F32((rows * n) ** -0.5)
+
+    barrier = pltpu.get_barrier_semaphore()
+    for partner in partners:
+        pl.semaphore_signal(
+            barrier, inc=1, device_id={"seq": partner}, device_id_type=pl.DeviceIdType.MESH
+        )
+
+    def remote(src, dst, sems, i, level):
+        return pltpu.make_async_remote_copy(
+            src_ref=src, dst_ref=dst, send_sem=sems.at[0, i], recv_sem=sems.at[1, i],
+            device_id={"seq": partners[level]}, device_id_type=pl.DeviceIdType.MESH,
+        )
+
+    def span(c):
+        return pl.ds(pl.multiple_of(c * size, size), size)
+
+    def p_copy(c):
+        return remote(p_send.at[span(c)], p_recv.at[span(c)], p_sems, c, -1)
+
+    def q_copy(c):
+        return remote(q.at[span(c)], q_recv.at[span(c)], q_sems, c, -1)
+
+    def first_part(c):
+        r = span(c)
+        x = x_ref[r, :].astype(F32)
+        mean = jnp.mean(x, axis=-1, keepdims=True)
+        mid = x - mean
+        inv = lax.rsqrt(jnp.mean(mid * mid, axis=-1, keepdims=True) + 1e-05)
+        value, grad = gelu_parts(mid * inv * gain_ref[...])
+        value = value.astype(BF16)
+        p_send[r, :] = dot(value, w_ref[far_tap]).astype(BF16)
+        act[r, :] = value
+        slope[r, :] = grad
+        mean_s[r, :] = mean
+        inv_s[r, :] = inv
+
+    first_part(0)
+    pl.semaphore_wait(barrier, len(bits))
+    p_copy(0).start()
+
+    @pl.loop(1, CHUNKS)
+    def _(c):
+        first_part(c)
+        p_copy(c).start()
+
+    @pl.loop(0, CHUNKS)
+    def _(c):
+        r = span(c)
+        own[r, :] = dot(act[r, :], w_ref[1])
+
+    @pl.loop(0, CHUNKS)
+    def _(c):
+        r = span(c)
+        grad_hid = dot_last(cot_ref[r, :], wp_ref[...])
+        p_copy(c).wait_recv()
+        value, grad = gelu_parts(own[r, :] + p_recv[r, :].astype(F32))
+        q[r, :] = (grad * grad_hid).astype(BF16)
+        q_copy(c).start()
+        value = value.astype(BF16)
+        hid[r, :] = value
+        out_ref[r, :] = (x_ref[r, :].astype(F32) + dot(value, wp_ref[...])).astype(BF16)
+
+    cut = n // 2
+    for j in range(2):
+        cols = slice(j * cut * shard, (j + 1) * cut * shard)
+        part = slice(j * cut, (j + 1) * cut)
+        early[part, :shard, :] = dot_rows(act[:, cols], q[...]).reshape(cut, shard, narrow)
+        early[part, shard:, :] = dot_rows(cot_ref[:, cols], hid[...]).reshape(cut, shard, narrow)
+
+    def send_half(level, cur, sends, recvs, sems):
+        count = n >> (level + 1)
+        base = n - 2 * count
+
+        @pl.loop(0, count)
+        def _(i):
+            sends[base + i] = cur[2 * i + 1 - mine[level]].astype(BF16)
+
+        copy = remote(
+            sends.at[pl.ds(base, count)], recvs.at[pl.ds(base, count)], sems, level, level
+        )
+        copy.start()
+        return copy
+
+    def add_half(level, cur, recvs, copy):
+        count = n >> (level + 1)
+        base = n - 2 * count
+        copy.wait_recv()
+
+        @pl.loop(0, count)
+        def _(i):
+            cur[i] = cur[2 * i + mine[level]] + recvs[base + i].astype(F32)
+
+    waits = []
+    last = len(bits) - 1
+
+    def back_part(c):
+        r = span(c)
+        grad_act = dot_last(q[r, :], w_ref[1]) + dot_last(q_recv[r, :], w_ref[far_tap])
+        inv = inv_s[r, :]
+        xhat = (x_ref[r, :].astype(F32) - mean_s[r, :]) * inv
+        gn = grad_act * slope[r, :]
+        gain_acc[...] += jnp.sum((gn * xhat).reshape(size // 8, 8, channels), axis=0)
+        gx = gn * gain_ref[...]
+        m1 = jnp.mean(gx, axis=-1, keepdims=True)
+        m2 = jnp.mean(gx * xhat, axis=-1, keepdims=True)
+        gin_ref[r, :] = (cot_ref[r, :].astype(F32) + inv * (gx - m1 - xhat * m2)).astype(BF16)
+
+    gain_acc[...] = jnp.zeros_like(gain_acc)
+    for level in range(last):
+        copy = send_half(level, early, e_send, e_recv, e_sems)
+        waits.append(copy)
+        q_copy(level).wait_recv()
+        if level < CHUNKS - 1:
+            back_part(level)
+        add_half(level, early, e_recv, copy)
+    e_last = send_half(last, early, e_send, e_recv, e_sems)
+    waits.append(e_last)
+    head = (CHUNKS - 1) * size
+
+    for j in range(2):
+        cols = slice(j * cut * shard, (j + 1) * cut * shard)
+        part = slice(j * cut, (j + 1) * cut)
+        late[part] = dot_rows(act[:head, cols], q_recv[:head, :]).reshape(cut, shard, narrow)
+    q_copy(CHUNKS - 1).wait_recv()
+    for j in range(2):
+        cols = slice(j * cut * shard, (j + 1) * cut * shard)
+        part = slice(j * cut, (j + 1) * cut)
+        late[part] += dot_rows(act[head:, cols], q_recv[head:, :]).reshape(cut, shard, narrow)
+    copy = send_half(0, late, l_send, l_recv, l_sems)
+    waits.append(copy)
+    back_part(CHUNKS - 1)
+
+    g_send[0] = gain_acc[...]
+    for level in range(len(bits)):
+        g_copy = remote(g_send.at[level], g_recv.at[level], g_sems, level, level)
+        g_copy.start()
+        waits.append(g_copy)
+        if level < last:
+            add_half(level, late, l_recv, copy)
+            copy = send_half(level + 1, late, l_send, l_recv, l_sems)
+            waits.append(copy)
+        g_copy.wait_recv()
+        total = g_send[level] + g_recv[level]
+        if level < last:
+            g_send[level + 1] = total
+        else:
+            gg_ref[...] = jnp.sum(total, axis=0, keepdims=True) * scale
+    add_half(last, early, e_recv, e_last)
+    gd_ref[1] = early[0, :shard, :] * scale
+    gp_ref[...] = early[0, shard:, :] * scale
+    copy.wait_recv()
+    gd_ref[far_tap] = late[mine[last]] * scale
+    gd_ref[2 - far_tap] = l_recv[n - 2].astype(F32) * scale
+
+    for copy in waits:
+        copy.wait_send()
+
+    @pl.loop(0, CHUNKS)
+    def _(c):
+        p_copy(c).wait_send()
+        q_copy(c).wait_send()
+
+
+def paired_device(inputs, gain, w_dilated, w_point, cotangent):
+    num_seqs, bins, channels = inputs.shape
+    narrow = w_point.shape[0]
+    n = lax.axis_size("seq")
+    rows, shard = num_seqs * bins, channels // n
+    levels = n.bit_length() - 1
+    vmem = pl.BlockSpec(memory_space=pltpu.VMEM)
+    dma = pltpu.SemaphoreType.DMA
+    wide, slim = (rows, channels), (rows, narrow)
+    outputs, grad_inputs, gd, gp, gg = pl.pallas_call(
+        lambda *refs: block_kernel(n, *refs),
+        out_shape=[
+            jax.ShapeDtypeStruct(wide, BF16),
+            jax.ShapeDtypeStruct(wide, BF16),
+            jax.ShapeDtypeStruct((3, shard, narrow), F32),
+            jax.ShapeDtypeStruct((shard, narrow), F32),
+            jax.ShapeDtypeStruct((1, channels), F32),
+        ],
+        in_specs=[vmem] * 5,
+        out_specs=[vmem] * 5,
+        scratch_shapes=[
+            pltpu.VMEM(wide, BF16),
+            pltpu.VMEM(slim, F32),
+            pltpu.VMEM(slim, BF16),
+            pltpu.VMEM(slim, BF16),
+            pltpu.VMEM(slim, BF16),
+            pltpu.VMEM(slim, BF16),
+            pltpu.VMEM(slim, BF16),
+            pltpu.VMEM(wide, F32),
+            pltpu.VMEM((rows, 1), F32),
+            pltpu.VMEM((rows, 1), F32),
+            pltpu.VMEM((n, 2 * shard, narrow), F32),
+            pltpu.VMEM((n, shard, narrow), F32),
+            pltpu.VMEM((8, channels), F32),
+            pltpu.VMEM((n, 2 * shard, narrow), BF16),
+            pltpu.VMEM((n, 2 * shard, narrow), BF16),
+            pltpu.VMEM((n, shard, narrow), BF16),
+            pltpu.VMEM((n, shard, narrow), BF16),
+            pltpu.VMEM((levels, 8, channels), F32),
+            pltpu.VMEM((levels, 8, channels), F32),
+            dma((2, CHUNKS)),
+            dma((2, CHUNKS)),
+            dma((2, levels)),
+            dma((2, levels)),
+            dma((2, levels)),
+        ],
+        compiler_params=pltpu.CompilerParams(
+            collective_id=0, has_side_effects=True, vmem_limit_bytes=56 * 1024 * 1024
+        ),
+    )(
+        inputs.reshape(wide), gain.reshape(1, channels), w_dilated, w_point,
+        cotangent.reshape(wide),
+    )
+    mine = lax.dynamic_slice(gg.reshape(-1), (lax.axis_index("seq") * shard,), (shard,))
+    return outputs.reshape(inputs.shape), grad_inputs.reshape(inputs.shape), gd, gp.T, mine
+
+
+def any_device(inputs, *rest):
+    paired = lax.axis_size("seq") * inputs.shape[1] == 2 * DILATION
+    return (paired_device if paired else per_device)(inputs, *rest)
+
 
 def solution(mesh):
     in_specs = (P("groups", "seq", None), P(), P(), P(), P("groups", "seq", None))
@@ -171,5 +430,5 @@
         P(("groups", "seq")),
     )
     return jax.shard_map(
-        per_device, mesh=mesh, in_specs=in_specs, out_specs=out_specs, check_vma=False
+        any_device, mesh=mesh, in_specs=in_specs, out_specs=out_specs, check_vma=False
     )

time: 123 us -> 104 us (0.85)
  Pallas kernels: 0 us -> 95.8 us
  waiting for transfers between devices: 55.2 us -> 0 us
  matrix products: 25.4 us -> 0 us
  other arithmetic: 17.5 us -> 0 us
  starting transfers between devices: 15.6 us -> 0 us
    pallas_call x0 -> x1, Pallas kernels: none -> 95.8 us  [paired_device(): pl.pallas_call(lambda *refs: block_kernel(n, *refs), out_shape=[jax.Shape...]
    ppermute x12 -> x0, waiting for transfers between devices: 55.2 us -> none  [swap(): return lax.ppermute(value, 'seq', [(s, s ^ bit) for s in range(n)])]
    dot_general x11 -> x0, matrix products: 25.4 us -> none  [the longest x4 14 us: dot_last(): lax.dot_general(a, b, (((1,), (1,)), ((), ())), preferred_element_type=F32)]
    ppermute x12 -> x0, starting transfers between devices: 15.6 us -> none  [swap(): return lax.ppermute(value, 'seq', [(s, s ^ bit) for s in range(n)])]
    convert_element_type x12 -> x0, other arithmetic: 6.78 us -> none  [the longest x2 2.63 us: per_device(): hid = gelu_fn(pre).astype(BF16)]
    another operation x4 -> x0, other arithmetic: 4.64 us -> none  [the longest x2 2.66 us: per_device(): grad_inputs = jnp.stack(grad_in)]
    reduce_sum x2 -> x0, other arithmetic: 2.4 us -> none  [the longest x1 1.8 us: normalize(): mid = x - jnp.mean(x, axis=-1, keepdims=True)]
    dot_general x1 -> x0, local copies, waits for them, and re-layouts: 1.63 us -> none  [dot_rows(): lax.dot_general(a, b, (((0,), (0,)), ((), ())), preferred_element_type=F32)]
  transfers between devices with their start and end apart: 12 -> 0, of which waited for: 7 -> 0; matrix products, arithmetic and copies ran while one was open for 31% -> 0% of each run, Pallas kernels for 0% -> 0%
where the time goes in v3:
time: 104 us
  Pallas kernels  95.8 us (92%)
  local copies, waits for them, and re-layouts  7.74 us (7%)
    pallas_call x1, Pallas kernels, paired_device(): pl.pallas_call(lambda *refs: block_kernel(n, *refs), out_shape=[jax.Shape...  95.8 us
    unnamed x10, local copies, waits for them, and re-layouts  5.24 us

profile of v3, /device:TPU:0, one launch (start us, length us, event | category | flops | bytes accessed | tf_op | source)
XLA Modules:
  0.0 104.2 jit_solution(18391309284233635089)
XLA Ops:
  0.6 1.3 %reshape.28.refs_1_ = f32[1,768]{1,0:T(1,128)} reshape(f32[768]{0:T(1024)} %param.6) | data formatting | bytes 6144 | tf_op jit(solution)/shard_map/reshape | solution.py:411
  1.9 95.8 %shard_map.92 = (bf16[1024,768]{1,0:T(8,128)(2,1)}, bf16[1024,768]{1,0:T(8,128)(2,1)}, f32[3,48,384]{2,1,0:T(8,128)}, f32[48,384]{1,0:T(8,128)}, f32[1,768]{1,0:T(1,128)}) custom-call(bf16[1024,768]{1,0:T(8,128)(2,1)} %bitcast.9, f32[1,768]{1,0:T(1,128)} %reshape.28.refs_1_, bf16[3,768,384]{2,1,0:T(8,128)(2,1)} %refs_2_.1, bf16[384,768]{1,0:T(8,128)(2,1)} %refs_3_.1, ...), custom_call_target="tpu_custom_call" | custom-call | tf_op jit(solution)/shard_map/pallas_call | solution.py:370
  97.7 1.2 %dynamic-slice_bitcast_fusion = f32[48]{0:T(128)} fusion(f32[1,768]{1,0:T(1,128)} %get-tuple-element.14, s32[]{:T(128)S(6)} %select_n.3), kind=kLoop, calls=%fused_computation | loop fusion | bytes 388 | tf_op jit(solution)/shard_map/dynamic_slice | solution.py:414
  99.0 0.0 copy-start
  99.0 2.8 %copy.14 = bf16[2,512,768]{2,1,0:T(8,128)(2,1)} copy(bf16[2,512,768]{2,1,0:T(8,128)(2,1)} %bitcast.8) | data formatting | bytes 3145728
  101.7 0.0 copy-done
  101.7 0.0 copy-start.1
  101.7 0.0 copy-start.2
  101.7 1.1 %copy.15 = bf16[2,512,768]{2,1,0:T(8,128)(2,1)} copy(bf16[2,512,768]{2,1,0:T(8,128)(2,1)S(1)} %bitcast.7) | data formatting | bytes 3145728
  102.9 0.0 copy-done.1
  102.9 0.7 copy.16
  103.6 0.0 copy-done.2
  103.6 0.6 copy.17
Async XLA Ops:
  99.0 2.8 %copy-start = (bf16[1024,768]{1,0:T(8,128)(2,1)S(1)}, bf16[1024,768]{1,0:T(8,128)(2,1)}, u32[]{:S(2)}) copy-start(bf16[1024,768]{1,0:T(8,128)(2,1)} %get-tuple-element.11) | copy-start | bytes 4718596
  101.7 1.1 %copy-start.1 = (f32[3,48,384]{2,1,0:T(8,128)S(1)}, f32[3,48,384]{2,1,0:T(8,128)}, u32[]{:S(2)}) copy-start(f32[3,48,384]{2,1,0:T(8,128)} %get-tuple-element.22) | copy-start | bytes 663556
  101.7 1.8 %copy-start.2 = (f32[48,384]{1,0:T(8,128)S(1)}, f32[48,384]{1,0:T(8,128)}, u32[]{:S(2)}) copy-start(f32[48,384]{1,0:T(8,128)} %get-tuple-element.13) | copy-start | bytes 221188

commit v4 on v3

--- a/solution.py
+++ b/solution.py
@@ -223,7 +223,7 @@
         mean = jnp.mean(x, axis=-1, keepdims=True)
         mid = x - mean
         inv = lax.rsqrt(jnp.mean(mid * mid, axis=-1, keepdims=True) + 1e-05)
-        value, grad = gelu_parts(mid * inv * gain_ref[...])
+        value, grad = gelu_parts(mid * inv * gain_ref[...].reshape(1, channels))
         value = value.astype(BF16)
         p_send[r, :] = dot(value, w_ref[far_tap]).astype(BF16)
         act[r, :] = value
@@ -297,7 +297,7 @@
         xhat = (x_ref[r, :].astype(F32) - mean_s[r, :]) * inv
         gn = grad_act * slope[r, :]
         gain_acc[...] += jnp.sum((gn * xhat).reshape(size // 8, 8, channels), axis=0)
-        gx = gn * gain_ref[...]
+        gx = gn * gain_ref[...].reshape(1, channels)
         m1 = jnp.mean(gx, axis=-1, keepdims=True)
         m2 = jnp.mean(gx * xhat, axis=-1, keepdims=True)
         gin_ref[r, :] = (cot_ref[r, :].astype(F32) + inv * (gx - m1 - xhat * m2)).astype(BF16)
@@ -307,12 +307,16 @@
         copy = send_half(level, early, e_send, e_recv, e_sems)
         waits.append(copy)
         q_copy(level).wait_recv()
-        if level < CHUNKS - 1:
-            back_part(level)
+        back_part(level)
         add_half(level, early, e_recv, copy)
     e_last = send_half(last, early, e_send, e_recv, e_sems)
     waits.append(e_last)
     head = (CHUNKS - 1) * size
+
+    @pl.loop(last, CHUNKS - 1)
+    def _(c):
+        q_copy(c).wait_recv()
+        back_part(c)
 
     for j in range(2):
         cols = slice(j * cut * shard, (j + 1) * cut * shard)
@@ -341,7 +345,11 @@
         if level < last:
             g_send[level + 1] = total
         else:
-            gg_ref[...] = jnp.sum(total, axis=0, keepdims=True) * scale
+            total = jnp.sum(total, axis=0, keepdims=True) * scale
+            picked = total[:, :shard]
+            for s in range(1, n):
+                picked = jnp.where(me == s, total[:, s * shard : (s + 1) * shard], picked)
+            gg_ref[...] = picked
     add_half(last, early, e_recv, e_last)
     gd_ref[1] = early[0, :shard, :] * scale
     gp_ref[...] = early[0, shard:, :] * scale
@@ -374,7 +382,7 @@
             jax.ShapeDtypeStruct(wide, BF16),
             jax.ShapeDtypeStruct((3, shard, narrow), F32),
             jax.ShapeDtypeStruct((shard, narrow), F32),
-            jax.ShapeDtypeStruct((1, channels), F32),
+            jax.ShapeDtypeStruct((1, shard), F32),
         ],
         in_specs=[vmem] * 5,
         out_specs=[vmem] * 5,
@@ -408,11 +416,28 @@
             collective_id=0, has_side_effects=True, vmem_limit_bytes=56 * 1024 * 1024
         ),
     )(
-        inputs.reshape(wide), gain.reshape(1, channels), w_dilated, w_point,
+        inputs.reshape(wide), gain, w_dilated, w_point,
         cotangent.reshape(wide),
     )
-    mine = lax.dynamic_slice(gg.reshape(-1), (lax.axis_index("seq") * shard,), (shard,))
-    return outputs.reshape(inputs.shape), grad_inputs.reshape(inputs.shape), gd, gp.T, mine
+    step = rows // 2
+    tall = pl.BlockSpec((step, channels), lambda i: (i, 0))
+    taps = pl.BlockSpec(gd.shape, lambda i: (0, 0, 0))
+    gains = pl.BlockSpec(gg.shape, lambda i: (0, 0))
+    outputs, grad_inputs, gd, gg = pl.pallas_call(
+        deliver,
+        grid=(2,),
+        out_shape=[jax.ShapeDtypeStruct(a.shape, a.dtype) for a in (outputs, grad_inputs, gd, gg)],
+        in_specs=[tall, tall, taps, gains],
+        out_specs=[tall, tall, taps, gains],
+    )(outputs, grad_inputs, gd, gg)
+    return (
+        outputs.reshape(inputs.shape), grad_inputs.reshape(inputs.shape), gd, gp.T, gg.reshape(-1)
+    )
+
+
+def deliver(*refs):
+    for source, target in zip(refs[:4], refs[4:]):
+        target[...] = source[...]
 
 
 def any_device(inputs, *rest):

time: 104 us -> 102 us (0.981)
  local copies, waits for them, and re-layouts: 7.74 us -> 0.64 us
  Pallas kernels: 95.8 us -> 100 us
    unnamed x10 -> x3, local copies, waits for them, and re-layouts: 5.24 us -> 0.64 us
    pallas_call x0 -> x1, Pallas kernels: none -> 3.3 us  [paired_device(): pl.pallas_call(deliver, grid=(2,), out_shape=[jax.ShapeDtypeStruct(a.shap...]
    reshape x1 -> x0, local copies, waits for them, and re-layouts: 1.27 us -> none  [paired_device(): gain.reshape(1, channels)]
    dynamic_slice x1 -> x0, local copies, waits for them, and re-layouts: 1.23 us -> none  [paired_device(): lax.dynamic_slice(gg.reshape(-1), (lax.axis_index('seq') * shard,), (shar...]
    pallas_call x1, Pallas kernels: 95.8 us -> 96.9 us  [paired_device(): pl.pallas_call(lambda *refs: block_kernel(n, *refs), out_shape=[jax.Shape...]
where the time goes in v4:
time: 102 us
  Pallas kernels  100 us (98%)
    pallas_call x1, Pallas kernels, paired_device(): pl.pallas_call(lambda *refs: block_kernel(n, *refs), out_shape=[jax.Shape...  96.9 us
    pallas_call x1, Pallas kernels, paired_device(): pl.pallas_call(deliver, grid=(2,), out_shape=[jax.ShapeDtypeStruct(a.shap...  3.3 us

profile of v4, /device:TPU:0, one launch (start us, length us, event | category | flops | bytes accessed | tf_op | source)
XLA Modules:
  0.0 101.5 jit_solution(13188843453194377344)
XLA Ops:
  0.6 96.9 %shard_map.92 = (bf16[1024,768]{1,0:T(8,128)(2,1)}, bf16[1024,768]{1,0:T(8,128)(2,1)}, f32[3,48,384]{2,1,0:T(8,128)}, f32[48,384]{1,0:T(8,128)}, f32[1,48]{1,0:T(1,128)}) custom-call(bf16[1024,768]{1,0:T(8,128)(2,1)} %bitcast.6, f32[768]{0:T(1024)} %refs_1_.1, bf16[3,768,384]{2,1,0:T(8,128)(2,1)} %refs_2_.1, bf16[384,768]{1,0:T(8,128)(2,1)} %refs_3_.1, ...), custom_call_target="tpu_custom_call" | custom-call | tf_op jit(solution)/shard_map/pallas_call | solution.py:378
  97.6 0.0 copy-start
  97.6 3.3 %shard_map.93 = (bf16[1024,768]{1,0:T(8,128)(2,1)}, bf16[1024,768]{1,0:T(8,128)(2,1)}, f32[3,48,384]{2,1,0:T(8,128)}, f32[1,48]{1,0:T(1,128)}) custom-call(bf16[1024,768]{1,0:T(8,128)(2,1)} %get-tuple-element.14.refs_0_, bf16[1024,768]{1,0:T(8,128)(2,1)} %get-tuple-element.15.refs_1_, f32[3,48,384]{2,1,0:T(8,128)} %get-tuple-element.16.refs_2_, ...), custom_call_target="tpu_custom_call" | custom-call | tf_op jit(solution)/shard_map/pallas_call | solution.py:426
  100.9 0.0 copy-done
  100.9 0.6 copy.11
Async XLA Ops:
  97.6 3.3 %copy-start = (f32[48,384]{1,0:T(8,128)S(1)}, f32[48,384]{1,0:T(8,128)}, u32[]{:S(2)}) copy-start(f32[48,384]{1,0:T(8,128)} %get-tuple-element.21) | copy-start | bytes 221188

commit v5 on v4

--- a/solution.py
+++ b/solution.py
@@ -340,6 +340,10 @@
             add_half(level, late, l_recv, copy)
             copy = send_half(level + 1, late, l_send, l_recv, l_sems)
             waits.append(copy)
+        if level == 0:
+            add_half(last, early, e_recv, e_last)
+            gd_ref[1] = early[0, :shard, :] * scale
+            gp_ref[...] = early[0, shard:, :] * scale
         g_copy.wait_recv()
         total = g_send[level] + g_recv[level]
         if level < last:
@@ -350,9 +354,6 @@
             for s in range(1, n):
                 picked = jnp.where(me == s, total[:, s * shard : (s + 1) * shard], picked)
             gg_ref[...] = picked
-    add_half(last, early, e_recv, e_last)
-    gd_ref[1] = early[0, :shard, :] * scale
-    gp_ref[...] = early[0, shard:, :] * scale
     copy.wait_recv()
     gd_ref[far_tap] = late[mine[last]] * scale
     gd_ref[2 - far_tap] = l_recv[n - 2].astype(F32) * scale

time: 102 us -> 102 us (level)
  no operation moved by 1% of the time
where the time goes in v5:
time: 102 us; the launch traced here: 101 us
  Pallas kernels  100 us (98%)
    pallas_call x1, Pallas kernels, paired_device(): pl.pallas_call(lambda *refs: block_kernel(n, *refs), out_shape=[jax.Shape...  96.9 us
    pallas_call x1, Pallas kernels, paired_device(): pl.pallas_call(deliver, grid=(2,), out_shape=[jax.ShapeDtypeStruct(a.shap...  3.3 us

profile of v5, /device:TPU:0, one launch (start us, length us, event | category | flops | bytes accessed | tf_op | source)
XLA Modules:
  0.0 101.5 jit_solution(179047642129345402)
XLA Ops:
  0.6 96.9 %shard_map.92 = (bf16[1024,768]{1,0:T(8,128)(2,1)}, bf16[1024,768]{1,0:T(8,128)(2,1)}, f32[3,48,384]{2,1,0:T(8,128)}, f32[48,384]{1,0:T(8,128)}, f32[1,48]{1,0:T(1,128)}) custom-call(bf16[1024,768]{1,0:T(8,128)(2,1)} %bitcast.6, f32[768]{0:T(1024)} %refs_1_.1, bf16[3,768,384]{2,1,0:T(8,128)(2,1)} %refs_2_.1, bf16[384,768]{1,0:T(8,128)(2,1)} %refs_3_.1, ...), custom_call_target="tpu_custom_call" | custom-call | tf_op jit(solution)/shard_map/pallas_call | solution.py:379
  97.5 0.0 copy-start
  97.5 3.3 %shard_map.93 = (bf16[1024,768]{1,0:T(8,128)(2,1)}, bf16[1024,768]{1,0:T(8,128)(2,1)}, f32[3,48,384]{2,1,0:T(8,128)}, f32[1,48]{1,0:T(1,128)}) custom-call(bf16[1024,768]{1,0:T(8,128)(2,1)} %get-tuple-element.14.refs_0_, bf16[1024,768]{1,0:T(8,128)(2,1)} %get-tuple-element.15.refs_1_, f32[3,48,384]{2,1,0:T(8,128)} %get-tuple-element.16.refs_2_, ...), custom_call_target="tpu_custom_call" | custom-call | tf_op jit(solution)/shard_map/pallas_call | solution.py:427
  100.8 0.0 copy-done
  100.8 0.6 copy.11
Async XLA Ops:
  97.5 3.3 %copy-start = (f32[48,384]{1,0:T(8,128)S(1)}, f32[48,384]{1,0:T(8,128)}, u32[]{:S(2)}) copy-start(f32[48,384]{1,0:T(8,128)} %get-tuple-element.21) | copy-start | bytes 221188
